TPU v7x, 128 devices: a whole 4x4x4 slice. The times are simulated.
128 devices in a mesh: chain: 16 (over z, x), tp: 8 (over y, core).
Axes of the slice: x: 4, y: 4, z: 4, core: 2. Of those that a mesh axis runs over, the one named last changes fastest.
Arguments:
- tokens: bfloat16 [4096, 7168], P('chain', 'tp'), may hold values from -6 to 6
- w_down_q: bfloat16 [7168, 1536], P('tp'), may hold values from -0.0625 to 0.0625
- w_down_kv: bfloat16 [7168, 576], P('tp'), may hold values from -0.0625 to 0.0625
- q_gain: float32 [1536], replicated, may hold values from 0.1 to 1.9
- kv_gain: float32 [512], replicated, may hold values from 0.1 to 1.9
- w_up_q: bfloat16 [1536, 12288], P(None, 'tp'), may hold values from -0.15625 to 0.15625
- w_absorb: bfloat16 [64, 128, 512], P('tp')
- w_value: bfloat16 [64, 512, 128], P('tp'), may hold values from -0.25 to 0.25
- slot_block: int32 [32], P('chain'), may hold values from 0 to 31, each once
Outputs:
- attended: bfloat16 [4096, 8192], P('chain', 'tp')
- latent_cache: bfloat16 [32, 128, 576], P('chain', 'tp')
Inputs may be any that keep to these rules, and one draw needn't show every extreme that they name: `slot_block`: every prompt block is named by exactly one slot.
All inputs are finite; a program needn't handle non-finite values.
Results may differ from a plain program's by a relative error of at most 0.04.
Values may be sent and summed in bfloat16 or wider, within the bound.
A program may use at most 128 MiB of HBM per device.

v0:
```python
import functools
import math

import jax
import jax.numpy as jnp
import numpy as np
from jax import lax
from jax.experimental import pallas as pl
from jax.experimental.pallas import tpu as pltpu
from jax.sharding import PartitionSpec as P

MESH = pl.DeviceIdType.MESH
ROPE_BASE = 50000.0
FLOOR_SCORE = -1e30
QL, LAT, ROPE, NOPE, VH, HEADS = 1536, 512, 64, 128, 128, 8
SUMMED = LAT + 16
KEYW = 640
KV = LAT + ROPE
SCALE2 = (NOPE + ROPE) ** -0.5 * math.log2(math.e)
NT = (((1,), (1,)), ((), ()))
N_SEND = 80
RINGS = (
    (0, 0), (3, 0), (1, 0), (0, 3), (0, 1), (2, 0), (3, 3), (3, 1), (1, 3), (1, 1), (0, 2),
    (2, 3), (2, 1), (3, 2), (1, 2), (2, 2),
)


def rotary_tables():
    inverse = ROPE_BASE ** (-2.0 * np.arange(ROPE // 2) / ROPE)
    angles = np.arange(4096)[:, None] * inverse[None, :]
    cosine = np.concatenate([np.cos(angles), np.cos(angles)], 1)
    sine = np.concatenate([-np.sin(angles), np.sin(angles)], 1)
    both = np.concatenate([cosine, sine], 1).astype(np.float32)
    return both.reshape(16, 8, 2, 16, 2 * ROPE)


def rotate(values, table):
    half = ROPE // 2
    swapped = jnp.concatenate([values[:, half:], values[:, :half]], 1)
    return values * table[:, :ROPE] + swapped * table[:, ROPE:]


def normalize(values, gain):
    return values * lax.rsqrt(jnp.mean(values * values, -1, keepdims=True) + 1e-06) * gain


def kernel(
    tok_h, wq_h, wkv_h, qg_h, kvg_h, wu_h, wa_h, wv_h, slot_ref, tab_h,
    out_h, cache_ref,
    tok, wq, wkv, qg, kvg, wu, wa, wv, tabk, tabq,
    psk, pok, prk, psq, poq, prq, rks, rkr, rqs, rqr, cs, cq, kb, kt, qt, wat, wvt, first, acc, mx, ob,
    load_sem, send_sem, sib_sem, rk_sem, rq_sem, cq_sem, ky_sem, kp_sem, ks_sem, out_sem, own_sem,
):
    chain = lax.axis_index("chain")
    tp = lax.axis_index("tp")
    z, x = chain // 4, chain % 4
    y, core = tp // 2, tp % 2
    other = 1 - core
    mirror = 15 - chain
    half = chain // 8
    piece = core * 4 + y
    yp, ym, yf = (y + 1) % 4, (y + 3) % 4, (y + 2) % 4
    sibling = {"chain": chain, "tp": 2 * y + other}
    up = {"chain": chain, "tp": 2 * yp + core}
    down = {"chain": chain, "tp": 2 * ym + core}
    pair = {"chain": mirror, "tp": tp}
    a = x + core * (z - x)
    b = z + core * (x - z)
    stride_a, stride_b = 1 + 3 * core, 4 - 3 * core

    def at(da, db):
        return ((a + da) % 4) * stride_a + ((b + db) % 4) * stride_b

    ap = {"chain": at(1, 0), "tp": tp}
    am = {"chain": at(3, 0), "tp": tp}
    bp = {"chain": at(0, 1), "tp": tp}
    bm = {"chain": at(0, 3), "tp": tp}

    loads = {}
    for k, (name, src, dst) in enumerate(
        [
            ("tok", tok_h, tok), ("wkv", wkv_h, wkv), ("wq", wq_h, wq), ("kvg", kvg_h, kvg),
            ("qg", qg_h, qg), ("tabk", tab_h.at[chain, piece], tabk), ("wa", wa_h, wa),
            ("wu", wu_h, wu), ("wv", wv_h, wv), ("tab0", tab_h.at[chain, :, half], tabq.at[0]),
            ("tab1", tab_h.at[mirror, :, half], tabq.at[1]),
        ]
    ):
        loads[name] = pltpu.make_async_copy(src, dst, load_sem.at[k])
        if k < 6:
            loads[name].start()

    def loaded(*names):
        for name in names:
            loads[name].wait()

    barrier = pltpu.get_barrier_semaphore()
    partners = (sibling, up, down, pair, ap, am, bp, bm)
    for device in partners:
        pl.semaphore_signal(barrier, inc=1, device_id=device, device_id_type=MESH)
    pl.semaphore_wait(barrier, len(partners))

    sent = []

    def send(src, dst, recv, device):
        copy = pltpu.make_async_remote_copy(
            src_ref=src, dst_ref=dst, send_sem=send_sem.at[len(sent)], recv_sem=recv,
            device_id=device, device_id_type=MESH,
        )
        copy.start()
        sent.append(copy)

    def arrived(dst, recv):
        pltpu.make_async_remote_copy(
            src_ref=dst, dst_ref=dst, send_sem=send_sem.at[0], recv_sem=recv,
            device_id=sibling, device_id_type=MESH,
        ).wait_recv()

    def rows_of(c):
        return tok[pl.ds(pl.multiple_of(c * 128, 128), 128), :]

    def project_keys(c, dst):
        dst[...] = lax.dot_general(rows_of(c), wkv[...], NT, preferred_element_type=jnp.float32)

    def project_queries(c, dst):
        left = rows_of(c)

        def tile(i, _):
            cols = pl.ds(pl.multiple_of(i * 512, 512), 512)
            dst[:, cols] = jnp.dot(left, wq[:, cols], preferred_element_type=jnp.float32)
            return 0

        lax.fori_loop(0, 3, tile, 0)

    def ring_of(own, got, out, came, sems):
        def part(yy, h):
            rows = pl.ds(pl.multiple_of(yy * 32 + h * 16, 16), 16)
            return own[rows, :] + got[rows, :]

        def push(k, value, device):
            out[k] = value.astype(out.dtype)
            send(out.at[k], came.at[k], sems.at[k], device)

        def start():
            push(0, part(yf, 0), up)
            push(1, part(yf, 1), down)
            push(2, part(yp, 1), up)
            push(3, part(ym, 0), down)

        def middle():
            arrived(came.at[0], sems.at[0])
            push(4, part(yp, 0) + came[0].astype(jnp.float32), up)
            arrived(came.at[1], sems.at[1])
            push(5, part(ym, 1) + came[1].astype(jnp.float32), down)

        def end():
            for k in (2, 3, 4, 5):
                arrived(came.at[k], sems.at[k])
            totals = []
            for h, first, second in ((0, 4, 3), (1, 2, 5)):
                total = part(y, h) + came[first].astype(jnp.float32)
                totals.append(total + came[second].astype(jnp.float32))
            return totals

        return start, middle, end

    keys_start, keys_middle, keys_end = ring_of(pok, prk, rks, rkr, rk_sem)
    queries_start, queries_middle, queries_end = ring_of(poq, prq, rqs, rqr, rq_sem)

    loaded("tok", "wkv")
    project_keys(other, psk)
    send(psk, prk, sib_sem.at[0], sibling)
    project_keys(core, pok)
    loaded("wq")
    for name in ("wa", "wu", "wv", "tab0", "tab1"):
        loads[name].start()
    project_queries(other, psq)
    send(psq, prq, sib_sem.at[1], sibling)
    arrived(prk, sib_sem.at[0])
    keys_start()
    project_queries(core, poq)
    keys_middle()
    arrived(prq, sib_sem.at[1])
    queries_start()

    loaded("wa")

    def turn_absorb(h, _):
        wat[h] = wa[h].T
        return 0

    lax.fori_loop(0, HEADS, turn_absorb, 0)

    slot_own = 2 * chain + core

    def keys_y(yy, h, n):
        return kb.at[slot_own, pl.ds(pl.multiple_of(yy * 32 + h * 16, 16), n)]

    loaded("kvg", "tabk")
    gain_kv = jnp.concatenate([kvg[k : k + 1, :] for k in range(LAT // 128)], 1)
    for h, total in enumerate(keys_end()):
        latent = normalize(total[:, :LAT], gain_kv)
        turned = rotate(total[:, LAT:], tabk[h])
        rows = pl.ds(pl.multiple_of(y * 32 + h * 16, 16), 16)
        kb[slot_own, rows, :LAT] = latent.astype(jnp.bfloat16)
        kb[slot_own, rows, LAT:] = jnp.concatenate(
            [turned, jnp.zeros_like(turned)], 1
        ).astype(jnp.bfloat16)
    for k, device in enumerate((up, down)):
        send(keys_y(y, 0, 32), keys_y(y, 0, 32), ky_sem.at[k], device)
    queries_middle()
    arrived(keys_y(ym, 0, 32), ky_sem.at[0])
    send(keys_y(ym, 0, 16), keys_y(ym, 0, 16), ky_sem.at[2], up)
    arrived(keys_y(yp, 0, 32), ky_sem.at[1])
    send(keys_y(yp, 1, 16), keys_y(yp, 1, 16), ky_sem.at[3], down)

    def block(n, p=None):
        if p is None:
            return kb.at[2 * n + core]
        return kb.at[2 * n + core, pl.ds(64 * p, 64)]

    def pass_on(n, *devices):
        for device in devices:
            send(block(n), block(n), kp_sem.at[n, 0], device)
        send(block(n), block(n), ks_sem.at[n], sibling)

    def pass_part(n, p, device):
        send(block(n, p), block(n, p), kp_sem.at[n, p], device)

    def turn(n, side):
        cols = pl.ds(pl.multiple_of((n % 4) * 256 + side * 128, 128), 128)
        kt[n // 4, :LAT, cols] = kb[2 * n + side, :, :LAT].T

    def turn_own(steps):
        for u, v in steps:
            turn(at(u, v), core)

    def turn_other(steps):
        for u, v in steps:
            n = at(u, v)
            arrived(kb.at[2 * n + other], ks_sem.at[n])
            turn(n, other)

    def whole(n):
        arrived(block(n), kp_sem.at[n, 0])

    def halves(n):
        for p in range(2):
            arrived(block(n, p), kp_sem.at[n, p])

    def relay(u, v):
        n = at(u, v)
        if v == 2 or (u, v) == (2, 0):
            halves(n)
        else:
            whole(n)
        if v == 0:
            if u != 2:
                pass_part(n, 0 if u == 3 else 1, ap if u == 3 else am)
            pass_on(n, bp, bm)
        else:
            if v != 2:
                pass_part(n, 0 if v == 3 else 1, bp if v == 3 else bm)
            pass_on(n)

    arrived(keys_y(yf, 0, 16), ky_sem.at[2])
    arrived(keys_y(yf, 1, 16), ky_sem.at[3])
    pass_on(at(0, 0), ap, am, bp, bm)
    turn_own(RINGS[:1])

    loaded("qg")
    gain_q = jnp.concatenate([qg[k : k + 1, :] for k in range(QL // 128)], 1)
    for h, total in enumerate(queries_end()):
        cs[h] = normalize(total, gain_q).astype(jnp.bfloat16)

    def give(s, p, *devices):
        for device in devices:
            send(cq.at[s, p], cq.at[s, p], cq_sem.at[s, p], device)

    def take(s, p):
        arrived(cq.at[s, p], cq_sem.at[s, p])

    send(cs.at[1 - half], cq.at[1, piece], cq_sem.at[1, piece], pair)
    cq[0, piece] = cs[half]
    give(0, piece, up, down, sibling)
    pm, pp, pf = core * 4 + ym, core * 4 + yp, core * 4 + yf
    for u, v in RINGS[1:5]:
        relay(u, v)
    take(1, piece)
    give(1, piece, up, down, sibling)
    turn_own(RINGS[1:5])
    turn_other(RINGS[:1])
    take(0, pm)
    give(0, pm, up, sibling)
    take(0, pp)
    give(0, pp, sibling)
    take(1, pp)
    give(1, pp, down, sibling)
    take(1, pm)
    give(1, pm, sibling)
    for u, v in RINGS[5:11]:
        relay(u, v)
    turn_other(RINGS[1:5])
    loaded("wv")

    def turn_value(h, _):
        wvt[h] = wv[h].T
        return 0

    lax.fori_loop(0, HEADS, turn_value, 0)
    take(0, pf)
    give(0, pf, sibling)
    take(1, pf)
    give(1, pf, sibling)
    for s in range(2):
        for yy in range(4):
            take(s, other * 4 + yy)

    loaded("wu", "tab0", "tab1")

    def expand(i, _):
        cols = pl.ds(pl.multiple_of(i * 384, 384), 384)
        rows = cq[...].reshape(256, QL)
        projected = jnp.dot(rows, wu[:, cols], preferred_element_type=jnp.float32)
        table = tabq[...].reshape(256, 2 * ROPE)
        for j in range(2):
            head = 2 * i + j
            base = j * (NOPE + ROPE)
            nope = projected[:, base : base + NOPE].astype(jnp.bfloat16)
            turned = rotate(projected[:, base + NOPE : base + NOPE + ROPE], table)
            turned = jnp.concatenate([turned, jnp.zeros_like(turned)], 1).astype(jnp.bfloat16).T
            absorbed = jnp.dot(wat[head], nope.T, preferred_element_type=jnp.float32)
            absorbed = absorbed.astype(jnp.bfloat16)
            places = pl.ds(pl.multiple_of(head * 128, 128), 128)
            for s in range(2):
                qt[s, :LAT, places] = absorbed[:, s * 128 : s * 128 + 128]
                qt[s, LAT:, places] = turned[:, s * 128 : s * 128 + 128]
        return 0

    expand(0, 0)
    turn_own(RINGS[5:11])
    expand(1, 0)
    for u, v in RINGS[11:15]:
        relay(u, v)
    expand(2, 0)
    turn_own(RINGS[11:15])
    for u, v in RINGS[5:11]:
        arrived(kb.at[2 * at(u, v) + other], ks_sem.at[at(u, v)])
    expand(3, 0)
    for u, v in RINGS[5:11]:
        turn(at(u, v), other)
    acc[...] = jnp.zeros_like(acc)
    kt[:, LAT:, :] = jnp.ones((4, SUMMED - LAT, 1024), jnp.bfloat16)
    mx[...] = jnp.full_like(mx, FLOOR_SCORE)

    def turn(n, side):
        cols = pl.ds(pl.multiple_of((n % 4) * 256 + side * 128, 128), 128)
        kt[n // 4, :LAT, cols] = kb[2 * n + side, :, :LAT].T

    def turn_own(steps):
        for u, v in steps:
            turn(at(u, v), core)

    def turn_other(steps):
        for u, v in steps:
            n = at(u, v)
            arrived(kb.at[2 * n + other], ks_sem.at[n])
            turn(n, other)

    def whole(n):
        arrived(block(n), kp_sem.at[n, 0])

    def halves(n):
        for p in range(2):
            arrived(block(n, p), kp_sem.at[n, p])

    relay(2, 2)
    turn_own(RINGS[15:])
    turn_other(RINGS[11:])
    for j in range(2):
        rows = pl.ds(pl.multiple_of(tp * 16, 16), 16)
        cache_ref[j] = kb[slot_ref[j], rows, :][:, :KV]

    token = lax.broadcasted_iota(jnp.int32, (1, 256), 1) & 127
    place = ((token >> 4) << 5) + (token & 15) + half * 16
    key_iota = lax.broadcasted_iota(jnp.int32, (1024, 1), 0)

    def score(s, c, r, size):
        keys = kb[pl.ds(8 * c, size // 128)].reshape(size, KEYW)
        queries = qt[s, :, 256 * r : 256 * r + 256]
        return jnp.dot(keys, queries, preferred_element_type=jnp.float32)

    def chunk(s, c, blk, size, last):
        ahead = first[:size, :]
        for r in range(4):
            cols = slice(256 * r, 256 * r + 256)
            scores = ahead * SCALE2
            if r < 3:
                ahead = score(s, c, r + 1, size)
            elif not last:
                first[...] = score(s, c + 1, 0, size)
            if last:
                visible = key_iota[:size] + 1024 * c <= place + 256 * blk
                scores = jnp.where(visible, scores, FLOOR_SCORE)
            before = mx[s, :, cols]
            peak = jnp.maximum(before, jnp.max(scores, 0, keepdims=True))
            shrink = jnp.exp2(before - peak)
            weights = jnp.exp2(scores - peak).astype(jnp.bfloat16)
            mx[s, :, cols] = peak
            mixed = jnp.dot(kt[c, :, :size], weights, preferred_element_type=jnp.float32)
            acc[s, :, cols] = acc[s, :, cols] * shrink + mixed

    def attend(s, blk):
        first[...] = score(s, 0, 0, 1024)

        def step(c, _):
            chunk(s, c, blk, 1024, False)
            return 0

        lax.fori_loop(0, blk // 4, step, 0)

        @pl.when(blk % 4 >= 2)
        def _():
            chunk(s, blk // 4, blk, 1024, True)

        @pl.when(blk % 4 < 2)
        def _():
            chunk(s, blk // 4, blk, 512, True)

    def finish(s):
        def value_of(h, _):
            cols = pl.ds(pl.multiple_of(h * VH, VH), VH)
            mixed = acc[s, :LAT, cols] * (1.0 / acc[s, LAT : LAT + 1, cols])
            mixed = mixed.astype(jnp.bfloat16)
            value = jnp.dot(wvt[h], mixed, preferred_element_type=jnp.float32).T
            ob[s, :, :, cols] = value.astype(jnp.bfloat16).reshape(8, 16, VH)
            return 0

        lax.fori_loop(0, HEADS, value_of, 0)

    attend(1, mirror)
    finish(1)
    send(ob.at[1], out_h.at[:, half], out_sem.at[0], pair)
    attend(0, chain)
    finish(0)
    keep = pltpu.make_async_copy(ob.at[0], out_h.at[:, half], own_sem.at[0])
    keep.start()
    keep.wait()
    arrived(out_h.at[:, 1 - half], out_sem.at[0])
    for copy in sent:
        copy.wait_send()


def hand_over(att_h, cache_h, att_out, cache_out, att, cache, sem):
    pieces = [(cache_h, cache, cache_out)]
    for k in range(4):
        rows = pl.ds(64 * k, 64)
        pieces.append((att_h.at[rows], att.at[rows], att_out.at[rows]))
    into = [pltpu.make_async_copy(p[0], p[1], sem.at[0, k]) for k, p in enumerate(pieces)]
    out = [pltpu.make_async_copy(p[1], p[2], sem.at[1, k]) for k, p in enumerate(pieces)]
    for copy in into:
        copy.start()
    for first, second in zip(into, out):
        first.wait()
        second.start()
    for copy in out:
        copy.wait()


def per_device(tokens, w_down_q, w_down_kv, q_gain, kv_gain, w_up_q, w_absorb, w_value, slot_block):
    bf16, f32 = jnp.bfloat16, jnp.float32
    table = jnp.asarray(rotary_tables())
    hbm = pl.BlockSpec(memory_space=pl.ANY)
    dma = pltpu.SemaphoreType.DMA
    attended, cache = pl.pallas_call(
        kernel,
        out_shape=(
            jax.ShapeDtypeStruct((8, 2, 16, HEADS * VH), bf16),
            jax.ShapeDtypeStruct((2, 16, KV), bf16),
        ),
        in_specs=[hbm] * 8 + [pl.BlockSpec(memory_space=pltpu.SMEM), hbm],
        out_specs=(hbm, pl.BlockSpec(memory_space=pltpu.VMEM)),
        scratch_shapes=[
            pltpu.VMEM((256, 896), bf16),
            pltpu.VMEM((896, QL), bf16),
            pltpu.VMEM((KV, 896), bf16),
            pltpu.VMEM((QL // 128, 128), f32),
            pltpu.VMEM((LAT // 128, 128), f32),
            pltpu.VMEM((QL, HEADS * (NOPE + ROPE)), bf16),
            pltpu.VMEM((HEADS, NOPE, LAT), bf16),
            pltpu.VMEM((HEADS, LAT, VH), bf16),
            pltpu.VMEM((2, 16, 2 * ROPE), f32),
            pltpu.VMEM((2, 8, 16, 2 * ROPE), f32),
            pltpu.VMEM((128, KV), f32),
            pltpu.VMEM((128, KV), f32),
            pltpu.VMEM((128, KV), f32),
            pltpu.VMEM((128, QL), f32),
            pltpu.VMEM((128, QL), f32),
            pltpu.VMEM((128, QL), f32),
            pltpu.VMEM((6, 16, KV), bf16),
            pltpu.VMEM((6, 16, KV), bf16),
            pltpu.VMEM((6, 16, QL), f32),
            pltpu.VMEM((6, 16, QL), f32),
            pltpu.VMEM((2, 16, QL), bf16),
            pltpu.VMEM((2, 8, 16, QL), bf16),
            pltpu.VMEM((32, 128, KEYW), bf16),
            pltpu.VMEM((4, SUMMED, 1024), bf16),
            pltpu.VMEM((2, KEYW, HEADS * 128), bf16),
            pltpu.VMEM((HEADS, LAT, NOPE), bf16),
            pltpu.VMEM((HEADS, VH, LAT), bf16),
            pltpu.VMEM((1024, 256), f32),
            pltpu.VMEM((2, SUMMED, HEADS * 128), f32),
            pltpu.VMEM((2, 1, HEADS * 128), f32),
            pltpu.VMEM((2, 8, 16, HEADS * VH), bf16),
            dma((11,)),
            dma((N_SEND,)),
            dma((2,)),
            dma((6,)),
            dma((6,)),
            dma((2, 8)),
            dma((4,)),
            dma((16, 2)),
            dma((16,)),
            dma((1,)),
            dma((1,)),
        ],
        compiler_params=pltpu.CompilerParams(
            collective_id=0, has_side_effects=True, vmem_limit_bytes=56 * 2**20
        ),
    )(
        tokens, w_down_q, w_down_kv.T, q_gain.reshape(-1, 128), kv_gain.reshape(-1, 128),
        w_up_q, w_absorb, w_value, slot_block, table,
    )
    attended = attended.reshape(256, HEADS * VH)
    return pl.pallas_call(
        hand_over,
        out_shape=(
            jax.ShapeDtypeStruct(attended.shape, bf16),
            jax.ShapeDtypeStruct(cache.shape, bf16),
        ),
        in_specs=[hbm, hbm],
        out_specs=(hbm, hbm),
        scratch_shapes=[
            pltpu.VMEM(attended.shape, bf16),
            pltpu.VMEM(cache.shape, bf16),
            dma((2, 5)),
        ],
        compiler_params=pltpu.CompilerParams(vmem_limit_bytes=60 * 2**20),
    )(attended, cache)


def solution(mesh):
    placed = (
        P("chain", "tp"),
        P("tp", None),
        P("tp", None),
        P(),
        P(),
        P(None, "tp"),
        P("tp", None, None),
        P("tp", None, None),
        P("chain"),
    )
    return jax.shard_map(
        per_device,
        mesh=mesh,
        in_specs=placed,
        out_specs=(P("chain", "tp"), P("chain", "tp", None)),
        check_vma=False,
    )
```

profile of v0, /device:TPU:1, one launch (start us, length us, event | category | flops | bytes accessed | tf_op | source)
XLA Modules:
  0.0 75.2 jit_solution(14594410852788375788)
XLA Ops:
  0.6 72.6 %shard_map.113 = (bf16[8,2,16,1024]{3,2,1,0:T(8,128)(2,1)}, bf16[2,16,576]{2,1,0:T(8,128)(2,1)}) custom-call(bf16[256,896]{1,0:T(8,128)(2,1)} %tok_h.1, bf16[896,1536]{1,0:T(8,128)(2,1)} %wq_h.1, bf16[576,896]{1,0:T(8,128)(2,1)} %bitcast.4, f32[12,128]{1,0:T(8,128)} %bitcast.6, f32[4,128]{1,0:T(4,128)} %bitcast.7, bf16[1536,1536]{1,0:T(8,128)(2,1)} %wu_h.1, ...), custom_call_target="tpu_custom_call" | custom-call | tf_op jit(solution)/shard_map/pallas_call | solution.py:474
  73.2 1.9 %shard_map.114 = (bf16[256,1024]{1,0:T(8,128)(2,1)}, bf16[2,16,576]{2,1,0:T(8,128)(2,1)}) custom-call(bf16[256,1024]{1,0:T(8,128)(2,1)} %bitcast.5, bf16[2,16,576]{2,1,0:T(8,128)(2,1)} %get-tuple-element.5.cache_h), custom_call_target="tpu_custom_call" | custom-call | tf_op jit(solution)/shard_map/pallas_call | solution.py:534
where the time goes:
time: 75.6 us; the launch traced here: 75.2 us
  Pallas kernels  74.4 us (98%)
  between operations  0.8 us (1%)
    pallas_call x1, Pallas kernels, per_device(): pl.pallas_call(kernel, out_shape=(jax.ShapeDtypeStruct((8, 2, 16, HEADS *...  72.6 us
    pallas_call x1, Pallas kernels, per_device(): pl.pallas_call(hand_over, out_shape=(jax.ShapeDtypeStruct(attended.shape,...  1.86 us

commit v1 on v0

--- a/solution.py
+++ b/solution.py
@@ -13,7 +13,6 @@
 ROPE_BASE = 50000.0
 FLOOR_SCORE = -1e30
 QL, LAT, ROPE, NOPE, VH, HEADS = 1536, 512, 64, 128, 128, 8
-SUMMED = LAT + 16
 KEYW = 640
 KV = LAT + ROPE
 SCALE2 = (NOPE + ROPE) ** -0.5 * math.log2(math.e)
@@ -48,7 +47,7 @@
     tok_h, wq_h, wkv_h, qg_h, kvg_h, wu_h, wa_h, wv_h, slot_ref, tab_h,
     out_h, cache_ref,
     tok, wq, wkv, qg, kvg, wu, wa, wv, tabk, tabq,
-    psk, pok, prk, psq, poq, prq, rks, rkr, rqs, rqr, cs, cq, kb, kt, qt, wat, wvt, first, acc, mx, ob,
+    psk, pok, prk, psq, poq, prq, rks, rkr, rqs, rqr, cs, cq, kb, qb, first, acc, mx, tot, ob,
     load_sem, send_sem, sib_sem, rk_sem, rq_sem, cq_sem, ky_sem, kp_sem, ks_sem, out_sem, own_sem,
 ):
     chain = lax.axis_index("chain")
@@ -182,14 +181,6 @@
     arrived(prq, sib_sem.at[1])
     queries_start()
 
-    loaded("wa")
-
-    def turn_absorb(h, _):
-        wat[h] = wa[h].T
-        return 0
-
-    lax.fori_loop(0, HEADS, turn_absorb, 0)
-
     slot_own = 2 * chain + core
 
     def keys_y(yy, h, n):
@@ -226,20 +217,6 @@
     def pass_part(n, p, device):
         send(block(n, p), block(n, p), kp_sem.at[n, p], device)
 
-    def turn(n, side):
-        cols = pl.ds(pl.multiple_of((n % 4) * 256 + side * 128, 128), 128)
-        kt[n // 4, :LAT, cols] = kb[2 * n + side, :, :LAT].T
-
-    def turn_own(steps):
-        for u, v in steps:
-            turn(at(u, v), core)
-
-    def turn_other(steps):
-        for u, v in steps:
-            n = at(u, v)
-            arrived(kb.at[2 * n + other], ks_sem.at[n])
-            turn(n, other)
-
     def whole(n):
         arrived(block(n), kp_sem.at[n, 0])
 
@@ -265,7 +242,6 @@
     arrived(keys_y(yf, 0, 16), ky_sem.at[2])
     arrived(keys_y(yf, 1, 16), ky_sem.at[3])
     pass_on(at(0, 0), ap, am, bp, bm)
-    turn_own(RINGS[:1])
 
     loaded("qg")
     gain_q = jnp.concatenate([qg[k : k + 1, :] for k in range(QL // 128)], 1)
@@ -287,8 +263,6 @@
         relay(u, v)
     take(1, piece)
     give(1, piece, up, down, sibling)
-    turn_own(RINGS[1:5])
-    turn_other(RINGS[:1])
     take(0, pm)
     give(0, pm, up, sibling)
     take(0, pp)
@@ -299,14 +273,6 @@
     give(1, pm, sibling)
     for u, v in RINGS[5:11]:
         relay(u, v)
-    turn_other(RINGS[1:5])
-    loaded("wv")
-
-    def turn_value(h, _):
-        wvt[h] = wv[h].T
-        return 0
-
-    lax.fori_loop(0, HEADS, turn_value, 0)
     take(0, pf)
     give(0, pf, sibling)
     take(1, pf)
@@ -315,7 +281,7 @@
         for yy in range(4):
             take(s, other * 4 + yy)
 
-    loaded("wu", "tab0", "tab1")
+    loaded("wa", "wu", "tab0", "tab1")
 
     def expand(i, _):
         cols = pl.ds(pl.multiple_of(i * 384, 384), 384)
@@ -327,29 +293,21 @@
             base = j * (NOPE + ROPE)
             nope = projected[:, base : base + NOPE].astype(jnp.bfloat16)
             turned = rotate(projected[:, base + NOPE : base + NOPE + ROPE], table)
-            turned = jnp.concatenate([turned, jnp.zeros_like(turned)], 1).astype(jnp.bfloat16).T
-            absorbed = jnp.dot(wat[head], nope.T, preferred_element_type=jnp.float32)
+            turned = jnp.concatenate([turned, jnp.zeros_like(turned)], 1).astype(jnp.bfloat16)
+            absorbed = jnp.dot(nope, wa[head], preferred_element_type=jnp.float32)
             absorbed = absorbed.astype(jnp.bfloat16)
             places = pl.ds(pl.multiple_of(head * 128, 128), 128)
             for s in range(2):
-                qt[s, :LAT, places] = absorbed[:, s * 128 : s * 128 + 128]
-                qt[s, LAT:, places] = turned[:, s * 128 : s * 128 + 128]
+                qb[s, places, :LAT] = absorbed[s * 128 : s * 128 + 128]
+                qb[s, places, LAT:] = turned[s * 128 : s * 128 + 128]
         return 0
 
-    expand(0, 0)
-    turn_own(RINGS[5:11])
-    expand(1, 0)
+    lax.fori_loop(0, HEADS // 4, expand, 0)
     for u, v in RINGS[11:15]:
         relay(u, v)
-    expand(2, 0)
-    turn_own(RINGS[11:15])
-    for u, v in RINGS[5:11]:
-        arrived(kb.at[2 * at(u, v) + other], ks_sem.at[at(u, v)])
-    expand(3, 0)
-    for u, v in RINGS[5:11]:
-        turn(at(u, v), other)
+    lax.fori_loop(HEADS // 4, HEADS // 2, expand, 0)
     acc[...] = jnp.zeros_like(acc)
-    kt[:, LAT:, :] = jnp.ones((4, SUMMED - LAT, 1024), jnp.bfloat16)
+    tot[...] = jnp.zeros_like(tot)
     mx[...] = jnp.full_like(mx, FLOOR_SCORE)
 
     def turn(n, side):
@@ -374,40 +332,46 @@
             arrived(block(n, p), kp_sem.at[n, p])
 
     relay(2, 2)
-    turn_own(RINGS[15:])
-    turn_other(RINGS[11:])
+    for n in range(16):
+        arrived(kb.at[2 * n + other], ks_sem.at[n])
     for j in range(2):
         rows = pl.ds(pl.multiple_of(tp * 16, 16), 16)
         cache_ref[j] = kb[slot_ref[j], rows, :][:, :KV]
 
-    token = lax.broadcasted_iota(jnp.int32, (1, 256), 1) & 127
+    token = lax.broadcasted_iota(jnp.int32, (512, 1), 0) & 127
     place = ((token >> 4) << 5) + (token & 15) + half * 16
-    key_iota = lax.broadcasted_iota(jnp.int32, (1024, 1), 0)
+    key_iota = lax.broadcasted_iota(jnp.int32, (1, 1024), 1)
 
     def score(s, c, r, size):
         keys = kb[pl.ds(8 * c, size // 128)].reshape(size, KEYW)
-        queries = qt[s, :, 256 * r : 256 * r + 256]
-        return jnp.dot(keys, queries, preferred_element_type=jnp.float32)
+        queries = qb[s, 512 * r : 512 * r + 512, :]
+        return lax.dot_general(queries, keys, NT, preferred_element_type=jnp.float32)
 
     def chunk(s, c, blk, size, last):
-        ahead = first[:size, :]
-        for r in range(4):
-            cols = slice(256 * r, 256 * r + 256)
+        ahead = first[:, :size]
+        for r in range(2):
+            rows = slice(512 * r, 512 * r + 512)
             scores = ahead * SCALE2
-            if r < 3:
+            if r < 1:
                 ahead = score(s, c, r + 1, size)
             elif not last:
                 first[...] = score(s, c + 1, 0, size)
             if last:
-                visible = key_iota[:size] + 1024 * c <= place + 256 * blk
+                visible = key_iota[:, :size] + 1024 * c <= place + 256 * blk
                 scores = jnp.where(visible, scores, FLOOR_SCORE)
-            before = mx[s, :, cols]
-            peak = jnp.maximum(before, jnp.max(scores, 0, keepdims=True))
+            parts = [scores[:, k : k + 128] for k in range(0, size, 128)]
+            before = mx[s, rows, :]
+            top = jnp.max(functools.reduce(jnp.maximum, parts), 1, keepdims=True)
+            peak = jnp.maximum(before, top)
             shrink = jnp.exp2(before - peak)
-            weights = jnp.exp2(scores - peak).astype(jnp.bfloat16)
-            mx[s, :, cols] = peak
-            mixed = jnp.dot(kt[c, :, :size], weights, preferred_element_type=jnp.float32)
-            acc[s, :, cols] = acc[s, :, cols] * shrink + mixed
+            weights = [jnp.exp2(p - peak) for p in parts]
+            mx[s, rows, :] = peak
+            tot[s, rows, :] = tot[s, rows, :] * shrink + sum(weights[1:], weights[0])
+            weights = jnp.concatenate([w.astype(jnp.bfloat16) for w in weights], 1)
+            latent = kb[pl.ds(8 * c, size // 128), :, :LAT].reshape(size, LAT)
+            mixed = jnp.dot(weights, latent, preferred_element_type=jnp.float32)
+            shrink = jnp.concatenate([shrink] * (LAT // 128), 1)
+            acc[s, rows, :] = acc[s, rows, :] * shrink + mixed
 
     def attend(s, blk):
         first[...] = score(s, 0, 0, 1024)
@@ -429,15 +393,16 @@
     def finish(s):
         def value_of(h, _):
             cols = pl.ds(pl.multiple_of(h * VH, VH), VH)
-            mixed = acc[s, :LAT, cols] * (1.0 / acc[s, LAT : LAT + 1, cols])
-            mixed = mixed.astype(jnp.bfloat16)
-            value = jnp.dot(wvt[h], mixed, preferred_element_type=jnp.float32).T
+            total = jnp.sum(tot[s, cols, :], 1, keepdims=True)
+            mixed = (acc[s, cols, :] * (1.0 / total)).astype(jnp.bfloat16)
+            value = jnp.dot(mixed, wv[h], preferred_element_type=jnp.float32)
             ob[s, :, :, cols] = value.astype(jnp.bfloat16).reshape(8, 16, VH)
             return 0
 
         lax.fori_loop(0, HEADS, value_of, 0)
 
     attend(1, mirror)
+    loaded("wv")
     finish(1)
     send(ob.at[1], out_h.at[:, half], out_sem.at[0], pair)
     attend(0, chain)
@@ -503,13 +468,11 @@
             pltpu.VMEM((2, 16, QL), bf16),
             pltpu.VMEM((2, 8, 16, QL), bf16),
             pltpu.VMEM((32, 128, KEYW), bf16),
-            pltpu.VMEM((4, SUMMED, 1024), bf16),
-            pltpu.VMEM((2, KEYW, HEADS * 128), bf16),
-            pltpu.VMEM((HEADS, LAT, NOPE), bf16),
-            pltpu.VMEM((HEADS, VH, LAT), bf16),
-            pltpu.VMEM((1024, 256), f32),
-            pltpu.VMEM((2, SUMMED, HEADS * 128), f32),
-            pltpu.VMEM((2, 1, HEADS * 128), f32),
+            pltpu.VMEM((2, HEADS * 128, KEYW), bf16),
+            pltpu.VMEM((512, 1024), f32),
+            pltpu.VMEM((2, HEADS * 128, LAT), f32),
+            pltpu.VMEM((2, HEADS * 128, 128), f32),
+            pltpu.VMEM((2, HEADS * 128, 128), f32),
             pltpu.VMEM((2, 8, 16, HEADS * VH), bf16),
             dma((11,)),
             dma((N_SEND,)),

time: 75.6 us -> 74.4 us (0.984)
  Pallas kernels: 74.4 us -> 73.5 us
    pallas_call x1, Pallas kernels: 72.6 us -> 71.6 us  [per_device(): pl.pallas_call(kernel, out_shape=(jax.ShapeDtypeStruct((8, 2, 16, HEADS *...]
where the time goes in v1:
time: 74.4 us; the launch traced here: 74.3 us
  Pallas kernels  73.5 us (99%)
  between operations  0.8 us (1%)
    pallas_call x1, Pallas kernels, per_device(): pl.pallas_call(kernel, out_shape=(jax.ShapeDtypeStruct((8, 2, 16, HEADS *...  71.6 us
    pallas_call x1, Pallas kernels, per_device(): pl.pallas_call(hand_over, out_shape=(jax.ShapeDtypeStruct(attended.shape,...  1.86 us

profile of v1, /device:TPU:1, one launch (start us, length us, event | category | flops | bytes accessed | tf_op | source)
XLA Modules:
  0.0 74.3 jit_solution(322730384593715112)
XLA Ops:
  0.6 71.6 %shard_map.113 = (bf16[8,2,16,1024]{3,2,1,0:T(8,128)(2,1)}, bf16[2,16,576]{2,1,0:T(8,128)(2,1)}) custom-call(bf16[256,896]{1,0:T(8,128)(2,1)} %tok_h.1, bf16[896,1536]{1,0:T(8,128)(2,1)} %wq_h.1, bf16[576,896]{1,0:T(8,128)(2,1)} %bitcast.4, f32[12,128]{1,0:T(8,128)} %bitcast.6, f32[4,128]{1,0:T(4,128)} %bitcast.7, bf16[1536,1536]{1,0:T(8,128)(2,1)} %wu_h.1, ...), custom_call_target="tpu_custom_call" | custom-call | tf_op jit(solution)/shard_map/pallas_call | solution.py:439
  72.3 1.9 %shard_map.114 = (bf16[256,1024]{1,0:T(8,128)(2,1)}, bf16[2,16,576]{2,1,0:T(8,128)(2,1)}) custom-call(bf16[256,1024]{1,0:T(8,128)(2,1)} %bitcast.5, bf16[2,16,576]{2,1,0:T(8,128)(2,1)} %get-tuple-element.5.cache_h), custom_call_target="tpu_custom_call" | custom-call | tf_op jit(solution)/shard_map/pallas_call | solution.py:497

commit v2 on v1

--- a/solution.py
+++ b/solution.py
@@ -19,7 +19,7 @@
 NT = (((1,), (1,)), ((), ()))
 N_SEND = 80
 RINGS = (
-    (0, 0), (3, 0), (1, 0), (0, 3), (0, 1), (2, 0), (3, 3), (3, 1), (1, 3), (1, 1), (0, 2),
+    (0, 0), (3, 0), (1, 0), (0, 3), (0, 1), (2, 0), (0, 2), (3, 3), (3, 1), (1, 3), (1, 1),
     (2, 3), (2, 1), (3, 2), (1, 2), (2, 2),
 )
 
@@ -47,7 +47,7 @@
     tok_h, wq_h, wkv_h, qg_h, kvg_h, wu_h, wa_h, wv_h, slot_ref, tab_h,
     out_h, cache_ref,
     tok, wq, wkv, qg, kvg, wu, wa, wv, tabk, tabq,
-    psk, pok, prk, psq, poq, prq, rks, rkr, rqs, rqr, cs, cq, kb, qb, first, acc, mx, tot, ob,
+    psk, pok, prk, psq, poq, prq, rks, rkr, rqs, rqr, cs, cq, kb, qb, acc, mx, tot, ob,
     load_sem, send_sem, sib_sem, rk_sem, rq_sem, cq_sem, ky_sem, kp_sem, ks_sem, out_sem, own_sem,
 ):
     chain = lax.axis_index("chain")
@@ -101,12 +101,16 @@
     sent = []
 
     def send(src, dst, recv, device):
-        copy = pltpu.make_async_remote_copy(
-            src_ref=src, dst_ref=dst, send_sem=send_sem.at[len(sent)], recv_sem=recv,
-            device_id=device, device_id_type=MESH,
-        )
-        copy.start()
-        sent.append(copy)
+        slot = len(sent)
+
+        def build():
+            return pltpu.make_async_remote_copy(
+                src_ref=src(), dst_ref=dst(), send_sem=send_sem.at[slot], recv_sem=recv(),
+                device_id=device, device_id_type=MESH,
+            )
+
+        build().start()
+        sent.append(build)
 
     def arrived(dst, recv):
         pltpu.make_async_remote_copy(
@@ -137,7 +141,7 @@
 
         def push(k, value, device):
             out[k] = value.astype(out.dtype)
-            send(out.at[k], came.at[k], sems.at[k], device)
+            send(lambda: out.at[k], lambda: came.at[k], lambda: sems.at[k], device)
 
         def start():
             push(0, part(yf, 0), up)
@@ -167,17 +171,17 @@
 
     loaded("tok", "wkv")
     project_keys(other, psk)
-    send(psk, prk, sib_sem.at[0], sibling)
+    send(lambda: psk, lambda: prk, lambda: sib_sem.at[0], sibling)
     project_keys(core, pok)
     loaded("wq")
     for name in ("wa", "wu", "wv", "tab0", "tab1"):
         loads[name].start()
-    project_queries(other, psq)
-    send(psq, prq, sib_sem.at[1], sibling)
     arrived(prk, sib_sem.at[0])
     keys_start()
+    project_queries(other, psq)
+    send(lambda: psq, lambda: prq, lambda: sib_sem.at[1], sibling)
+    keys_middle()
     project_queries(core, poq)
-    keys_middle()
     arrived(prq, sib_sem.at[1])
     queries_start()
 
@@ -196,13 +200,16 @@
         kb[slot_own, rows, LAT:] = jnp.concatenate(
             [turned, jnp.zeros_like(turned)], 1
         ).astype(jnp.bfloat16)
-    for k, device in enumerate((up, down)):
-        send(keys_y(y, 0, 32), keys_y(y, 0, 32), ky_sem.at[k], device)
+    def send_y(yy, h, n, k, device):
+        send(lambda: keys_y(yy, h, n), lambda: keys_y(yy, h, n), lambda: ky_sem.at[k], device)
+
+    send_y(y, 0, 32, 0, up)
+    send_y(y, 0, 32, 1, down)
     queries_middle()
     arrived(keys_y(ym, 0, 32), ky_sem.at[0])
-    send(keys_y(ym, 0, 16), keys_y(ym, 0, 16), ky_sem.at[2], up)
+    send_y(ym, 0, 16, 2, up)
     arrived(keys_y(yp, 0, 32), ky_sem.at[1])
-    send(keys_y(yp, 1, 16), keys_y(yp, 1, 16), ky_sem.at[3], down)
+    send_y(yp, 1, 16, 3, down)
 
     def block(n, p=None):
         if p is None:
@@ -211,11 +218,13 @@
 
     def pass_on(n, *devices):
         for device in devices:
-            send(block(n), block(n), kp_sem.at[n, 0], device)
-        send(block(n), block(n), ks_sem.at[n], sibling)
+            send(lambda: block(n), lambda: block(n), lambda: kp_sem.at[n, 0], device)
+        send(lambda: block(n), lambda: block(n), lambda: ks_sem.at[n], sibling)
 
     def pass_part(n, p, device):
-        send(block(n, p), block(n, p), kp_sem.at[n, p], device)
+        send(lambda: block(n, p), lambda: block(n, p), lambda: kp_sem.at[n, p], device)
+
+    places_of = {step: at(*step) for step in RINGS}
 
     def whole(n):
         arrived(block(n), kp_sem.at[n, 0])
@@ -225,7 +234,7 @@
             arrived(block(n, p), kp_sem.at[n, p])
 
     def relay(u, v):
-        n = at(u, v)
+        n = places_of[u, v]
         if v == 2 or (u, v) == (2, 0):
             halves(n)
         else:
@@ -250,12 +259,12 @@
 
     def give(s, p, *devices):
         for device in devices:
-            send(cq.at[s, p], cq.at[s, p], cq_sem.at[s, p], device)
+            send(lambda: cq.at[s, p], lambda: cq.at[s, p], lambda: cq_sem.at[s, p], device)
 
     def take(s, p):
         arrived(cq.at[s, p], cq_sem.at[s, p])
 
-    send(cs.at[1 - half], cq.at[1, piece], cq_sem.at[1, piece], pair)
+    send(lambda: cs.at[1 - half], lambda: cq.at[1, piece], lambda: cq_sem.at[1, piece], pair)
     cq[0, piece] = cs[half]
     give(0, piece, up, down, sibling)
     pm, pp, pf = core * 4 + ym, core * 4 + yp, core * 4 + yf
@@ -271,7 +280,7 @@
     give(1, pp, down, sibling)
     take(1, pm)
     give(1, pm, sibling)
-    for u, v in RINGS[5:11]:
+    for u, v in RINGS[5:7]:
         relay(u, v)
     take(0, pf)
     give(0, pf, sibling)
@@ -303,7 +312,7 @@
         return 0
 
     lax.fori_loop(0, HEADS // 4, expand, 0)
-    for u, v in RINGS[11:15]:
+    for u, v in RINGS[7:11]:
         relay(u, v)
     lax.fori_loop(HEADS // 4, HEADS // 2, expand, 0)
     acc[...] = jnp.zeros_like(acc)
@@ -331,13 +340,6 @@
         for p in range(2):
             arrived(block(n, p), kp_sem.at[n, p])
 
-    relay(2, 2)
-    for n in range(16):
-        arrived(kb.at[2 * n + other], ks_sem.at[n])
-    for j in range(2):
-        rows = pl.ds(pl.multiple_of(tp * 16, 16), 16)
-        cache_ref[j] = kb[slot_ref[j], rows, :][:, :KV]
-
     token = lax.broadcasted_iota(jnp.int32, (512, 1), 0) & 127
     place = ((token >> 4) << 5) + (token & 15) + half * 16
     key_iota = lax.broadcasted_iota(jnp.int32, (1, 1024), 1)
@@ -348,14 +350,12 @@
         return lax.dot_general(queries, keys, NT, preferred_element_type=jnp.float32)
 
     def chunk(s, c, blk, size, last):
-        ahead = first[:, :size]
+        ahead = score(s, c, 0, size)
         for r in range(2):
-            rows = slice(512 * r, 512 * r + 512)
+            rows = pl.ds(512 * r, 512)
             scores = ahead * SCALE2
             if r < 1:
                 ahead = score(s, c, r + 1, size)
-            elif not last:
-                first[...] = score(s, c + 1, 0, size)
             if last:
                 visible = key_iota[:, :size] + 1024 * c <= place + 256 * blk
                 scores = jnp.where(visible, scores, FLOOR_SCORE)
@@ -373,23 +373,6 @@
             shrink = jnp.concatenate([shrink] * (LAT // 128), 1)
             acc[s, rows, :] = acc[s, rows, :] * shrink + mixed
 
-    def attend(s, blk):
-        first[...] = score(s, 0, 0, 1024)
-
-        def step(c, _):
-            chunk(s, c, blk, 1024, False)
-            return 0
-
-        lax.fori_loop(0, blk // 4, step, 0)
-
-        @pl.when(blk % 4 >= 2)
-        def _():
-            chunk(s, blk // 4, blk, 1024, True)
-
-        @pl.when(blk % 4 < 2)
-        def _():
-            chunk(s, blk // 4, blk, 512, True)
-
     def finish(s):
         def value_of(h, _):
             cols = pl.ds(pl.multiple_of(h * VH, VH), VH)
@@ -401,18 +384,60 @@
 
         lax.fori_loop(0, HEADS, value_of, 0)
 
-    attend(1, mirror)
     loaded("wv")
-    finish(1)
-    send(ob.at[1], out_h.at[:, half], out_sem.at[0], pair)
-    attend(0, chain)
+
+    def row(j, _):
+        @pl.when(j == 1)
+        def _():
+            for u, v in RINGS[11:15]:
+                relay(u, v)
+
+        @pl.when(j == 3)
+        def _():
+            relay(2, 2)
+
+        c = (z + j + (j == 2).astype(jnp.int32) - (j == 3).astype(jnp.int32)) % 4
+        for k in range(4):
+            arrived(kb.at[2 * (4 * c + k) + other], ks_sem.at[4 * c + k])
+
+        def side(q, _):
+            s = 1 - q
+            blk = chain + s * (mirror - chain)
+            edge = blk // 4
+
+            @pl.when(c < edge)
+            def _():
+                chunk(s, c, blk, 1024, False)
+
+            @pl.when((c == edge) & (blk % 4 >= 2))
+            def _():
+                chunk(s, c, blk, 1024, True)
+
+            @pl.when((c == edge) & (blk % 4 < 2))
+            def _():
+                chunk(s, c, blk, 512, True)
+
+            @pl.when((j == 3) & (q == 0))
+            def _():
+                finish(1)
+                send(lambda: ob.at[1], lambda: out_h.at[:, half], lambda: out_sem.at[0], pair)
+
+            return 0
+
+        lax.fori_loop(0, 2, side, 0)
+        return 0
+
+    lax.fori_loop(0, 4, row, 0)
     finish(0)
     keep = pltpu.make_async_copy(ob.at[0], out_h.at[:, half], own_sem.at[0])
     keep.start()
+    for j in range(2):
+        rows = pl.ds(pl.multiple_of(tp * 16, 16), 16)
+        cache_ref[j] = kb[slot_ref[j], rows, :][:, :KV]
     keep.wait()
     arrived(out_h.at[:, 1 - half], out_sem.at[0])
-    for copy in sent:
-        copy.wait_send()
+    for build in sent:
+        build().wait_send()
 
 
 def hand_over(att_h, cache_h, att_out, cache_out, att, cache, sem):
@@ -469,7 +494,6 @@
             pltpu.VMEM((2, 8, 16, QL), bf16),
             pltpu.VMEM((32, 128, KEYW), bf16),
             pltpu.VMEM((2, HEADS * 128, KEYW), bf16),
-            pltpu.VMEM((512, 1024), f32),
             pltpu.VMEM((2, HEADS * 128, LAT), f32),
             pltpu.VMEM((2, HEADS * 128, 128), f32),
             pltpu.VMEM((2, HEADS * 128, 128), f32),

time: 74.4 us -> 77.5 us (1.042)
  Pallas kernels: 73.5 us -> 76.7 us
    pallas_call x1, Pallas kernels: 71.6 us -> 74.8 us  [per_device(): pl.pallas_call(kernel, out_shape=(jax.ShapeDtypeStruct((8, 2, 16, HEADS *...]
where the time goes in v2:
time: 77.5 us; the launch traced here: 77.3 us
  Pallas kernels  76.7 us (99%)
    pallas_call x1, Pallas kernels, per_device(): pl.pallas_call(kernel, out_shape=(jax.ShapeDtypeStruct((8, 2, 16, HEADS *...  74.8 us
    pallas_call x1, Pallas kernels, per_device(): pl.pallas_call(hand_over, out_shape=(jax.ShapeDtypeStruct(attended.shape,...  1.86 us

profile of v2, /device:TPU:1, one launch (start us, length us, event | category | flops | bytes accessed | tf_op | source)
XLA Modules:
  0.0 77.3 jit_solution(9334428447692581203)
XLA Ops:
  0.6 74.8 %shard_map.113 = (bf16[8,2,16,1024]{3,2,1,0:T(8,128)(2,1)}, bf16[2,16,576]{2,1,0:T(8,128)(2,1)}) custom-call(bf16[256,896]{1,0:T(8,128)(2,1)} %tok_h.1, bf16[896,1536]{1,0:T(8,128)(2,1)} %wq_h.1, bf16[576,896]{1,0:T(8,128)(2,1)} %bitcast.4, f32[12,128]{1,0:T(8,128)} %bitcast.6, f32[4,128]{1,0:T(4,128)} %bitcast.7, bf16[1536,1536]{1,0:T(8,128)(2,1)} %wu_h.1, ...), custom_call_target="tpu_custom_call" | custom-call | tf_op jit(solution)/shard_map/pallas_call | solution.py:464
  75.5 1.9 %shard_map.114 = (bf16[256,1024]{1,0:T(8,128)(2,1)}, bf16[2,16,576]{2,1,0:T(8,128)(2,1)}) custom-call(bf16[256,1024]{1,0:T(8,128)(2,1)} %bitcast.5, bf16[2,16,576]{2,1,0:T(8,128)(2,1)} %get-tuple-element.5.cache_h), custom_call_target="tpu_custom_call" | custom-call | tf_op jit(solution)/shard_map/pallas_call | solution.py:521

commit v3 on v2

--- a/solution.py
+++ b/solution.py
@@ -47,8 +47,8 @@
     tok_h, wq_h, wkv_h, qg_h, kvg_h, wu_h, wa_h, wv_h, slot_ref, tab_h,
     out_h, cache_ref,
     tok, wq, wkv, qg, kvg, wu, wa, wv, tabk, tabq,
-    psk, pok, prk, psq, poq, prq, rks, rkr, rqs, rqr, cs, cq, kb, qb, acc, mx, tot, ob,
-    load_sem, send_sem, sib_sem, rk_sem, rq_sem, cq_sem, ky_sem, kp_sem, ks_sem, out_sem, own_sem,
+    psk, pok, prk, psq, poq, prq, rks, rkr, rqs, rqr, cs, cq, kb, qb, first, second, acc, mx, tot, ob,
+    load_sem, send_sem, sib_sem, rk_sem, rq_sem, cq_sem, ky_sem, kp_sem, ks_sem, out_sem, outs_sem, own_sem,
 ):
     chain = lax.axis_index("chain")
     tp = lax.axis_index("tp")
@@ -98,19 +98,21 @@
         pl.semaphore_signal(barrier, inc=1, device_id=device, device_id_type=MESH)
     pl.semaphore_wait(barrier, len(partners))
 
-    sent = []
-
-    def send(src, dst, recv, device):
-        slot = len(sent)
-
-        def build():
-            return pltpu.make_async_remote_copy(
-                src_ref=src(), dst_ref=dst(), send_sem=send_sem.at[slot], recv_sem=recv(),
-                device_id=device, device_id_type=MESH,
-            )
-
-        build().start()
-        sent.append(build)
+    sent = {}
+
+    def send(src, dst, recv, device, key=None):
+        if key is None or key not in sent:
+            slot = len(sent)
+
+            def build():
+                return pltpu.make_async_remote_copy(
+                    src_ref=src(), dst_ref=dst(), send_sem=send_sem.at[slot], recv_sem=recv(),
+                    device_id=device, device_id_type=MESH,
+                )
+
+            key = slot if key is None else key
+            sent[key] = build
+        sent[key]().start()
 
     def arrived(dst, recv):
         pltpu.make_async_remote_copy(
@@ -184,6 +186,9 @@
     project_queries(core, poq)
     arrived(prq, sib_sem.at[1])
     queries_start()
+    acc[...] = jnp.zeros_like(acc)
+    tot[...] = jnp.zeros_like(tot)
+    mx[...] = jnp.full_like(mx, FLOOR_SCORE)
 
     slot_own = 2 * chain + core
 
@@ -216,13 +221,13 @@
             return kb.at[2 * n + core]
         return kb.at[2 * n + core, pl.ds(64 * p, 64)]
 
-    def pass_on(n, *devices):
-        for device in devices:
-            send(lambda: block(n), lambda: block(n), lambda: kp_sem.at[n, 0], device)
-        send(lambda: block(n), lambda: block(n), lambda: ks_sem.at[n], sibling)
-
-    def pass_part(n, p, device):
-        send(lambda: block(n, p), lambda: block(n, p), lambda: kp_sem.at[n, p], device)
+    def pass_on(step, n, *devices):
+        for k, device in enumerate(devices):
+            send(lambda: block(n), lambda: block(n), lambda: kp_sem.at[n, 0], device, (step, k))
+        send(lambda: block(n), lambda: block(n), lambda: ks_sem.at[n], sibling, (step, 4))
+
+    def pass_part(step, n, p, device):
+        send(lambda: block(n, p), lambda: block(n, p), lambda: kp_sem.at[n, p], device, (step, 5))
 
     places_of = {step: at(*step) for step in RINGS}
 
@@ -241,16 +246,16 @@
             whole(n)
         if v == 0:
             if u != 2:
-                pass_part(n, 0 if u == 3 else 1, ap if u == 3 else am)
-            pass_on(n, bp, bm)
+                pass_part((u, v), n, 0 if u == 3 else 1, ap if u == 3 else am)
+            pass_on((u, v), n, bp, bm)
         else:
             if v != 2:
-                pass_part(n, 0 if v == 3 else 1, bp if v == 3 else bm)
-            pass_on(n)
+                pass_part((u, v), n, 0 if v == 3 else 1, bp if v == 3 else bm)
+            pass_on((u, v), n)
 
     arrived(keys_y(yf, 0, 16), ky_sem.at[2])
     arrived(keys_y(yf, 1, 16), ky_sem.at[3])
-    pass_on(at(0, 0), ap, am, bp, bm)
+    pass_on((0, 0), places_of[0, 0], ap, am, bp, bm)
 
     loaded("qg")
     gain_q = jnp.concatenate([qg[k : k + 1, :] for k in range(QL // 128)], 1)
@@ -315,9 +320,21 @@
     for u, v in RINGS[7:11]:
         relay(u, v)
     lax.fori_loop(HEADS // 4, HEADS // 2, expand, 0)
-    acc[...] = jnp.zeros_like(acc)
-    tot[...] = jnp.zeros_like(tot)
-    mx[...] = jnp.full_like(mx, FLOOR_SCORE)
+
+    def meet(c):
+        for k in range(4):
+            n = 4 * (c % 4) + k
+            arrived(kb.at[2 * n + other], ks_sem.at[n])
+
+    def second_rows():
+        for u, v in RINGS[11:15]:
+            relay(u, v)
+        meet(z + 1)
+        meet(z + 3)
+
+    def last_row():
+        relay(2, 2)
+        meet(z + 2)
 
     def turn(n, side):
         cols = pl.ds(pl.multiple_of((n % 4) * 256 + side * 128, 128), 128)
@@ -342,101 +359,128 @@
 
     token = lax.broadcasted_iota(jnp.int32, (512, 1), 0) & 127
     place = ((token >> 4) << 5) + (token & 15) + half * 16
-    key_iota = lax.broadcasted_iota(jnp.int32, (1, 1024), 1)
-
-    def score(s, c, r, size):
-        keys = kb[pl.ds(8 * c, size // 128)].reshape(size, KEYW)
-        queries = qb[s, 512 * r : 512 * r + 512, :]
-        return lax.dot_general(queries, keys, NT, preferred_element_type=jnp.float32)
-
-    def chunk(s, c, blk, size, last):
-        ahead = score(s, c, 0, size)
-        for r in range(2):
-            rows = pl.ds(512 * r, 512)
-            scores = ahead * SCALE2
-            if r < 1:
-                ahead = score(s, c, r + 1, size)
-            if last:
-                visible = key_iota[:, :size] + 1024 * c <= place + 256 * blk
-                scores = jnp.where(visible, scores, FLOOR_SCORE)
-            parts = [scores[:, k : k + 128] for k in range(0, size, 128)]
-            before = mx[s, rows, :]
-            top = jnp.max(functools.reduce(jnp.maximum, parts), 1, keepdims=True)
-            peak = jnp.maximum(before, top)
-            shrink = jnp.exp2(before - peak)
-            weights = [jnp.exp2(p - peak) for p in parts]
-            mx[s, rows, :] = peak
-            tot[s, rows, :] = tot[s, rows, :] * shrink + sum(weights[1:], weights[0])
-            weights = jnp.concatenate([w.astype(jnp.bfloat16) for w in weights], 1)
-            latent = kb[pl.ds(8 * c, size // 128), :, :LAT].reshape(size, LAT)
-            mixed = jnp.dot(weights, latent, preferred_element_type=jnp.float32)
-            shrink = jnp.concatenate([shrink] * (LAT // 128), 1)
-            acc[s, rows, :] = acc[s, rows, :] * shrink + mixed
-
-    def finish(s):
-        def value_of(h, _):
-            cols = pl.ds(pl.multiple_of(h * VH, VH), VH)
-            total = jnp.sum(tot[s, cols, :], 1, keepdims=True)
-            mixed = (acc[s, cols, :] * (1.0 / total)).astype(jnp.bfloat16)
-            value = jnp.dot(mixed, wv[h], preferred_element_type=jnp.float32)
-            ob[s, :, :, cols] = value.astype(jnp.bfloat16).reshape(8, 16, VH)
-            return 0
-
-        lax.fori_loop(0, HEADS, value_of, 0)
+    key_iota = lax.broadcasted_iota(jnp.int32, (1, 512), 1)
+    early = 1 - z // 2
+    n_own, n_far = chain // 2 + 1, mirror // 2 + 1
+    ends = (n_own + early * (n_far - n_own), n_own + n_far, 18 - n_own, 18)
+    ends = (ends[0], ends[0] + n_far, ends[2], ends[3])
+    own_steps = 2 - (1 - early) * (1 - (chain % 4) // 2)
+
+    def plan(t):
+        p1 = (t >= ends[0]).astype(jnp.int32)
+        p2 = (t >= ends[1]).astype(jnp.int32)
+        p3 = (t >= ends[2]).astype(jnp.int32)
+        p = p1 + p2 + p3
+        j = t - p1 * ends[0] - p2 * (ends[1] - ends[0]) - p3 * (ends[2] - ends[1])
+        s = jnp.where(p == 0, early, jnp.where(p == 1, 1, jnp.where(p == 2, 1 - early, 0)))
+        r = jnp.where(p == 0, 0, jnp.where(p == 1, early, jnp.where(p == 2, 1 - early, 1)))
+        chunks = n_own + s * (n_far - n_own)
+        ahead = (2 * z + j) % chunks
+        back = chunks - 1 - j
+        c = back + s * early * (ahead - back)
+        return s, r, c, c == chunks - 1
+
+    def rows_of_pass(r):
+        return pl.ds(pl.multiple_of(r * 512, 512), 512)
+
+    def score(t, dst):
+        s, r, c, _ = plan(t)
+        keys = kb[pl.ds(4 * c, 4)].reshape(512, KEYW)
+        dst[...] = lax.dot_general(
+            qb[s, rows_of_pass(r), :], keys, NT, preferred_element_type=jnp.float32
+        )
+
+    def hide(t, dst):
+        s, _, c, last = plan(t)
+
+        @pl.when(last)
+        def _():
+            blk = chain + s * (mirror - chain)
+            visible = key_iota + 512 * c <= place + 256 * blk
+            dst[...] = jnp.where(visible, dst[...], FLOOR_SCORE)
+
+    def out_cols(r):
+        return pl.ds(pl.multiple_of(r * 512, 512), 512)
+
+    def out_copy(r):
+        return pltpu.make_async_remote_copy(
+            src_ref=ob.at[1, :, :, out_cols(r)], dst_ref=out_h.at[:, half, :, out_cols(r)],
+            send_sem=outs_sem.at[r], recv_sem=out_sem.at[r], device_id=pair, device_id_type=MESH,
+        )
+
+    def own_copy(r):
+        return pltpu.make_async_copy(
+            ob.at[0, :, :, out_cols(r)], out_h.at[:, half, :, out_cols(r)], own_sem.at[r]
+        )
+
+    def step(t, now, later):
+        s, r, c, _ = plan(t)
+        rows = rows_of_pass(r)
+        score(jnp.minimum(t + 1, 17), later)
+        parts = [now[:, k : k + 128] * SCALE2 for k in range(0, 512, 128)]
+        before = mx[s, rows, :]
+        top = jnp.max(functools.reduce(jnp.maximum, parts), 1, keepdims=True)
+        peak = jnp.maximum(before, top)
+        shrink = jnp.exp2(before - peak)
+        weights = [jnp.exp2(p - peak) for p in parts]
+        mx[s, rows, :] = peak
+        tot[s, rows, :] = tot[s, rows, :] * shrink + sum(weights[1:], weights[0])
+        weights = jnp.concatenate([w.astype(jnp.bfloat16) for w in weights], 1)
+        latent = kb[pl.ds(4 * c, 4), :, :LAT].reshape(512, LAT)
+        mixed = jnp.dot(weights, latent, preferred_element_type=jnp.float32)
+        shrink = jnp.concatenate([shrink] * (LAT // 128), 1)
+        acc[s, rows, :] = acc[s, rows, :] * shrink + mixed
+        hide(jnp.minimum(t + 1, 17), later)
+
+        @pl.when((t + 1 == ends[0]) | (t + 1 == ends[1]) | (t + 1 == ends[2]) | (t + 1 == ends[3]))
+        def _():
+            for k in range(4):
+                part = pl.ds(pl.multiple_of(r * 512 + k * 128, 128), 128)
+                total = jnp.sum(tot[s, part, :], 1, keepdims=True)
+                mixed = (acc[s, part, :] * (1.0 / total)).astype(jnp.bfloat16)
+                value = jnp.dot(mixed, wv[4 * r + k], preferred_element_type=jnp.float32)
+                ob[s, :, :, part] = value.astype(jnp.bfloat16).reshape(8, 16, VH)
+
+            @pl.when(s == 1)
+            def _():
+                out_copy(r).start()
+
+            @pl.when(s == 0)
+            def _():
+                own_copy(r).start()
 
     loaded("wv")
-
-    def row(j, _):
-        @pl.when(j == 1)
+    meet(z)
+    score(0, first)
+    hide(0, first)
+
+    def two_steps(i, _):
+        @pl.when((i == 0) & (own_steps == 1))
         def _():
-            for u, v in RINGS[11:15]:
-                relay(u, v)
-
-        @pl.when(j == 3)
+            second_rows()
+
+        @pl.when(i == 1)
         def _():
-            relay(2, 2)
-
-        c = (z + j + (j == 2).astype(jnp.int32) - (j == 3).astype(jnp.int32)) % 4
-        for k in range(4):
-            arrived(kb.at[2 * (4 * c + k) + other], ks_sem.at[4 * c + k])
-
-        def side(q, _):
-            s = 1 - q
-            blk = chain + s * (mirror - chain)
-            edge = blk // 4
-
-            @pl.when(c < edge)
-            def _():
-                chunk(s, c, blk, 1024, False)
-
-            @pl.when((c == edge) & (blk % 4 >= 2))
-            def _():
-                chunk(s, c, blk, 1024, True)
-
-            @pl.when((c == edge) & (blk % 4 < 2))
-            def _():
-                chunk(s, c, blk, 512, True)
-
-            @pl.when((j == 3) & (q == 0))
-            def _():
-                finish(1)
-                send(lambda: ob.at[1], lambda: out_h.at[:, half], lambda: out_sem.at[0], pair)
-
-            return 0
-
-        lax.fori_loop(0, 2, side, 0)
+            last_row()
+
+        step(2 * i, first, second)
+
+        @pl.when((i == 0) & (own_steps == 2))
+        def _():
+            second_rows()
+
+        step(2 * i + 1, second, first)
         return 0
 
-    lax.fori_loop(0, 4, row, 0)
-    finish(0)
-    keep = pltpu.make_async_copy(ob.at[0], out_h.at[:, half], own_sem.at[0])
-    keep.start()
+    lax.fori_loop(0, 9, two_steps, 0)
     for j in range(2):
         rows = pl.ds(pl.multiple_of(tp * 16, 16), 16)
         cache_ref[j] = kb[slot_ref[j], rows, :][:, :KV]
-    keep.wait()
-    arrived(out_h.at[:, 1 - half], out_sem.at[0])
-    for build in sent:
+    for r in range(2):
+        own_copy(r).wait()
+        out_copy(r).wait_send()
+        arrived(out_h.at[:, 1 - half, :, out_cols(r)], out_sem.at[r])
+    for build in sent.values():
         build().wait_send()
 
 
@@ -494,6 +538,8 @@
             pltpu.VMEM((2, 8, 16, QL), bf16),
             pltpu.VMEM((32, 128, KEYW), bf16),
             pltpu.VMEM((2, HEADS * 128, KEYW), bf16),
+            pltpu.VMEM((512, 512), f32),
+            pltpu.VMEM((512, 512), f32),
             pltpu.VMEM((2, HEADS * 128, LAT), f32),
             pltpu.VMEM((2, HEADS * 128, 128), f32),
             pltpu.VMEM((2, HEADS * 128, 128), f32),
@@ -507,8 +553,9 @@
             dma((4,)),
             dma((16, 2)),
             dma((16,)),
-            dma((1,)),
-            dma((1,)),
+            dma((2,)),
+            dma((2,)),
+            dma((2,)),
         ],
         compiler_params=pltpu.CompilerParams(
             collective_id=0, has_side_effects=True, vmem_limit_bytes=56 * 2**20

time: 77.5 us -> 74.2 us (0.957)
  Pallas kernels: 76.7 us -> 73.4 us
    pallas_call x1, Pallas kernels: 74.8 us -> 71.5 us  [per_device(): pl.pallas_call(kernel, out_shape=(jax.ShapeDtypeStruct((8, 2, 16, HEADS *...]
where the time goes in v3:
time: 74.2 us; the launch traced here: 74 us
  Pallas kernels  73.4 us (99%)
    pallas_call x1, Pallas kernels, per_device(): pl.pallas_call(kernel, out_shape=(jax.ShapeDtypeStruct((8, 2, 16, HEADS *...  71.5 us
    pallas_call x1, Pallas kernels, per_device(): pl.pallas_call(hand_over, out_shape=(jax.ShapeDtypeStruct(attended.shape,...  1.86 us

profile of v3, /device:TPU:1, one launch (start us, length us, event | category | flops | bytes accessed | tf_op | source)
XLA Modules:
  0.0 74.0 jit_solution(16211711845390560185)
XLA Ops:
  0.6 71.5 %shard_map.113 = (bf16[8,2,16,1024]{3,2,1,0:T(8,128)(2,1)}, bf16[2,16,576]{2,1,0:T(8,128)(2,1)}) custom-call(bf16[256,896]{1,0:T(8,128)(2,1)} %tok_h.1, bf16[896,1536]{1,0:T(8,128)(2,1)} %wq_h.1, bf16[576,896]{1,0:T(8,128)(2,1)} %bitcast.4, f32[12,128]{1,0:T(8,128)} %bitcast.6, f32[4,128]{1,0:T(4,128)} %bitcast.7, bf16[1536,1536]{1,0:T(8,128)(2,1)} %wu_h.1, ...), custom_call_target="tpu_custom_call" | custom-call | tf_op jit(solution)/shard_map/pallas_call | solution.py:508
  72.2 1.9 %shard_map.114 = (bf16[256,1024]{1,0:T(8,128)(2,1)}, bf16[2,16,576]{2,1,0:T(8,128)(2,1)}) custom-call(bf16[256,1024]{1,0:T(8,128)(2,1)} %bitcast.5, bf16[2,16,576]{2,1,0:T(8,128)(2,1)} %get-tuple-element.5.cache_h), custom_call_target="tpu_custom_call" | custom-call | tf_op jit(solution)/shard_map/pallas_call | solution.py:568

commit v4 on v3

--- a/solution.py
+++ b/solution.py
@@ -255,7 +255,6 @@
 
     arrived(keys_y(yf, 0, 16), ky_sem.at[2])
     arrived(keys_y(yf, 1, 16), ky_sem.at[3])
-    pass_on((0, 0), places_of[0, 0], ap, am, bp, bm)
 
     loaded("qg")
     gain_q = jnp.concatenate([qg[k : k + 1, :] for k in range(QL // 128)], 1)
@@ -273,24 +272,21 @@
     cq[0, piece] = cs[half]
     give(0, piece, up, down, sibling)
     pm, pp, pf = core * 4 + ym, core * 4 + yp, core * 4 + yf
-    for u, v in RINGS[1:5]:
-        relay(u, v)
-    take(1, piece)
-    give(1, piece, up, down, sibling)
     take(0, pm)
     give(0, pm, up, sibling)
     take(0, pp)
     give(0, pp, sibling)
+    take(1, piece)
+    give(1, piece, up, down, sibling)
     take(1, pp)
     give(1, pp, down, sibling)
     take(1, pm)
     give(1, pm, sibling)
-    for u, v in RINGS[5:7]:
-        relay(u, v)
     take(0, pf)
     give(0, pf, sibling)
     take(1, pf)
     give(1, pf, sibling)
+    pass_on((0, 0), places_of[0, 0], ap, am, bp, bm)
     for s in range(2):
         for yy in range(4):
             take(s, other * 4 + yy)
@@ -317,9 +313,11 @@
         return 0
 
     lax.fori_loop(0, HEADS // 4, expand, 0)
-    for u, v in RINGS[7:11]:
+    for u, v in RINGS[1:5]:
         relay(u, v)
     lax.fori_loop(HEADS // 4, HEADS // 2, expand, 0)
+    for u, v in RINGS[5:11]:
+        relay(u, v)
 
     def meet(c):
         for k in range(4):

time: 74.2 us -> 79.9 us (1.077)
  Pallas kernels: 73.4 us -> 79.2 us
    pallas_call x1, Pallas kernels: 71.5 us -> 77.3 us  [per_device(): pl.pallas_call(kernel, out_shape=(jax.ShapeDtypeStruct((8, 2, 16, HEADS *...]
where the time goes in v4:
time: 79.9 us; the launch traced here: 79.8 us
  Pallas kernels  79.2 us (99%)
    pallas_call x1, Pallas kernels, per_device(): pl.pallas_call(kernel, out_shape=(jax.ShapeDtypeStruct((8, 2, 16, HEADS *...  77.3 us
    pallas_call x1, Pallas kernels, per_device(): pl.pallas_call(hand_over, out_shape=(jax.ShapeDtypeStruct(attended.shape,...  1.86 us

profile of v4, /device:TPU:1, one launch (start us, length us, event | category | flops | bytes accessed | tf_op | source)
XLA Modules:
  0.0 79.8 jit_solution(741283310209208714)
XLA Ops:
  0.6 77.3 %shard_map.113 = (bf16[8,2,16,1024]{3,2,1,0:T(8,128)(2,1)}, bf16[2,16,576]{2,1,0:T(8,128)(2,1)}) custom-call(bf16[256,896]{1,0:T(8,128)(2,1)} %tok_h.1, bf16[896,1536]{1,0:T(8,128)(2,1)} %wq_h.1, bf16[576,896]{1,0:T(8,128)(2,1)} %bitcast.4, f32[12,128]{1,0:T(8,128)} %bitcast.6, f32[4,128]{1,0:T(4,128)} %bitcast.7, bf16[1536,1536]{1,0:T(8,128)(2,1)} %wu_h.1, ...), custom_call_target="tpu_custom_call" | custom-call | tf_op jit(solution)/shard_map/pallas_call | solution.py:506
  77.9 1.9 %shard_map.114 = (bf16[256,1024]{1,0:T(8,128)(2,1)}, bf16[2,16,576]{2,1,0:T(8,128)(2,1)}) custom-call(bf16[256,1024]{1,0:T(8,128)(2,1)} %bitcast.5, bf16[2,16,576]{2,1,0:T(8,128)(2,1)} %get-tuple-element.5.cache_h), custom_call_target="tpu_custom_call" | custom-call | tf_op jit(solution)/shard_map/pallas_call | solution.py:566

commit v5 on v3

--- a/solution.py
+++ b/solution.py
@@ -184,11 +184,6 @@
     send(lambda: psq, lambda: prq, lambda: sib_sem.at[1], sibling)
     keys_middle()
     project_queries(core, poq)
-    arrived(prq, sib_sem.at[1])
-    queries_start()
-    acc[...] = jnp.zeros_like(acc)
-    tot[...] = jnp.zeros_like(tot)
-    mx[...] = jnp.full_like(mx, FLOOR_SCORE)
 
     slot_own = 2 * chain + core
 
@@ -210,7 +205,8 @@
 
     send_y(y, 0, 32, 0, up)
     send_y(y, 0, 32, 1, down)
-    queries_middle()
+    arrived(prq, sib_sem.at[1])
+    queries_start()
     arrived(keys_y(ym, 0, 32), ky_sem.at[0])
     send_y(ym, 0, 16, 2, up)
     arrived(keys_y(yp, 0, 32), ky_sem.at[1])
@@ -256,6 +252,10 @@
     arrived(keys_y(yf, 0, 16), ky_sem.at[2])
     arrived(keys_y(yf, 1, 16), ky_sem.at[3])
     pass_on((0, 0), places_of[0, 0], ap, am, bp, bm)
+    queries_middle()
+    acc[...] = jnp.zeros_like(acc)
+    tot[...] = jnp.zeros_like(tot)
+    mx[...] = jnp.full_like(mx, FLOOR_SCORE)
 
     loaded("qg")
     gain_q = jnp.concatenate([qg[k : k + 1, :] for k in range(QL // 128)], 1)
@@ -360,38 +360,45 @@
     token = lax.broadcasted_iota(jnp.int32, (512, 1), 0) & 127
     place = ((token >> 4) << 5) + (token & 15) + half * 16
     key_iota = lax.broadcasted_iota(jnp.int32, (1, 512), 1)
-    early = 1 - z // 2
     n_own, n_far = chain // 2 + 1, mirror // 2 + 1
-    ends = (n_own + early * (n_far - n_own), n_own + n_far, 18 - n_own, 18)
-    ends = (ends[0], ends[0] + n_far, ends[2], ends[3])
-    own_steps = 2 - (1 - early) * (1 - (chain % 4) // 2)
+    first_z = (z == 0).astype(jnp.int32)
+    segments = []
+    for k, offset in enumerate((0, 1, 3, 2)):
+        c = (z + offset) % 4
+        segments.append((1, c, jnp.clip(n_far - 2 * c, 0, 2)))
+        segments.append((0, c, jnp.clip(n_own - 2 * c, 0, 2) * (1 - first_z * (k == 0))))
+    segments.append((0, z, jnp.clip(n_own - 2 * z, 0, 2) * first_z))
+    starts, final = [jnp.int32(0)], [jnp.int32(0), jnp.int32(0)]
+    for k, (s, _, chunks) in enumerate(segments):
+        starts.append(starts[-1] + 2 * chunks)
+        final[s] = jnp.where(chunks > 0, k, final[s])
 
     def plan(t):
-        p1 = (t >= ends[0]).astype(jnp.int32)
-        p2 = (t >= ends[1]).astype(jnp.int32)
-        p3 = (t >= ends[2]).astype(jnp.int32)
-        p = p1 + p2 + p3
-        j = t - p1 * ends[0] - p2 * (ends[1] - ends[0]) - p3 * (ends[2] - ends[1])
-        s = jnp.where(p == 0, early, jnp.where(p == 1, 1, jnp.where(p == 2, 1 - early, 0)))
-        r = jnp.where(p == 0, 0, jnp.where(p == 1, early, jnp.where(p == 2, 1 - early, 1)))
+        s, c, r, done = jnp.int32(0), jnp.int32(0), jnp.int32(0), jnp.int32(0)
+        for k, (side, row, chunks) in enumerate(segments):
+            inside = (t >= starts[k]) & (t < starts[k + 1])
+            place_in = t - starts[k]
+            pairs = chunks - 1
+            s = jnp.where(inside, side, s)
+            r = jnp.where(inside, jnp.where(chunks == 2, place_in // 2, place_in), r)
+            c = jnp.where(inside, 2 * row + pairs * (place_in % 2), c)
+            ended = (final[side] == k).astype(jnp.int32) * (1 - pairs * (1 - place_in % 2))
+            done = jnp.where(inside, ended, done)
         chunks = n_own + s * (n_far - n_own)
-        ahead = (2 * z + j) % chunks
-        back = chunks - 1 - j
-        c = back + s * early * (ahead - back)
-        return s, r, c, c == chunks - 1
+        return s, r, c, c == chunks - 1, done == 1
 
     def rows_of_pass(r):
         return pl.ds(pl.multiple_of(r * 512, 512), 512)
 
     def score(t, dst):
-        s, r, c, _ = plan(t)
+        s, r, c, _, _ = plan(t)
         keys = kb[pl.ds(4 * c, 4)].reshape(512, KEYW)
         dst[...] = lax.dot_general(
             qb[s, rows_of_pass(r), :], keys, NT, preferred_element_type=jnp.float32
         )
 
     def hide(t, dst):
-        s, _, c, last = plan(t)
+        s, _, c, last, _ = plan(t)
 
         @pl.when(last)
         def _():
@@ -414,7 +421,7 @@
         )
 
     def step(t, now, later):
-        s, r, c, _ = plan(t)
+        s, r, c, _, done = plan(t)
         rows = rows_of_pass(r)
         score(jnp.minimum(t + 1, 17), later)
         parts = [now[:, k : k + 128] * SCALE2 for k in range(0, 512, 128)]
@@ -432,7 +439,7 @@
         acc[s, rows, :] = acc[s, rows, :] * shrink + mixed
         hide(jnp.minimum(t + 1, 17), later)
 
-        @pl.when((t + 1 == ends[0]) | (t + 1 == ends[1]) | (t + 1 == ends[2]) | (t + 1 == ends[3]))
+        @pl.when(done)
         def _():
             for k in range(4):
                 part = pl.ds(pl.multiple_of(r * 512 + k * 128, 128), 128)
@@ -455,21 +462,18 @@
     hide(0, first)
 
     def two_steps(i, _):
-        @pl.when((i == 0) & (own_steps == 1))
-        def _():
-            second_rows()
-
-        @pl.when(i == 1)
-        def _():
-            last_row()
-
-        step(2 * i, first, second)
-
-        @pl.when((i == 0) & (own_steps == 2))
-        def _():
-            second_rows()
-
-        step(2 * i + 1, second, first)
+        for k, (now, later) in enumerate(((first, second), (second, first))):
+            t = 2 * i + k
+
+            @pl.when(t + 1 == starts[2])
+            def _():
+                second_rows()
+
+            @pl.when(t + 1 == starts[6])
+            def _():
+                last_row()
+
+            step(t, now, later)
         return 0
 
     lax.fori_loop(0, 9, two_steps, 0)

time: 74.2 us -> 74.9 us (level)
    pallas_call x1, Pallas kernels: 71.5 us -> 72.3 us  [per_device(): pl.pallas_call(kernel, out_shape=(jax.ShapeDtypeStruct((8, 2, 16, HEADS *...]
where the time goes in v5:
time: 74.9 us; the launch traced here: 74.8 us
  Pallas kernels  74.1 us (99%)
    pallas_call x1, Pallas kernels, per_device(): pl.pallas_call(kernel, out_shape=(jax.ShapeDtypeStruct((8, 2, 16, HEADS *...  72.3 us
    pallas_call x1, Pallas kernels, per_device(): pl.pallas_call(hand_over, out_shape=(jax.ShapeDtypeStruct(attended.shape,...  1.86 us

profile of v5, /device:TPU:1, one launch (start us, length us, event | category | flops | bytes accessed | tf_op | source)
XLA Modules:
  0.0 74.8 jit_solution(180928436525565182)
XLA Ops:
  0.6 72.3 %shard_map.113 = (bf16[8,2,16,1024]{3,2,1,0:T(8,128)(2,1)}, bf16[2,16,576]{2,1,0:T(8,128)(2,1)}) custom-call(bf16[256,896]{1,0:T(8,128)(2,1)} %tok_h.1, bf16[896,1536]{1,0:T(8,128)(2,1)} %wq_h.1, bf16[576,896]{1,0:T(8,128)(2,1)} %bitcast.4, f32[12,128]{1,0:T(8,128)} %bitcast.6, f32[4,128]{1,0:T(4,128)} %bitcast.7, bf16[1536,1536]{1,0:T(8,128)(2,1)} %wu_h.1, ...), custom_call_target="tpu_custom_call" | custom-call | tf_op jit(solution)/shard_map/pallas_call | solution.py:512
  72.9 1.9 %shard_map.114 = (bf16[256,1024]{1,0:T(8,128)(2,1)}, bf16[2,16,576]{2,1,0:T(8,128)(2,1)}) custom-call(bf16[256,1024]{1,0:T(8,128)(2,1)} %bitcast.5, bf16[2,16,576]{2,1,0:T(8,128)(2,1)} %get-tuple-element.5.cache_h), custom_call_target="tpu_custom_call" | custom-call | tf_op jit(solution)/shard_map/pallas_call | solution.py:572

commit v6 on v5

--- a/solution.py
+++ b/solution.py
@@ -357,7 +357,7 @@
         for p in range(2):
             arrived(block(n, p), kp_sem.at[n, p])
 
-    token = lax.broadcasted_iota(jnp.int32, (512, 1), 0) & 127
+    token = lax.broadcasted_iota(jnp.int32, (1024, 1), 0) & 127
     place = ((token >> 4) << 5) + (token & 15) + half * 16
     key_iota = lax.broadcasted_iota(jnp.int32, (1, 512), 1)
     n_own, n_far = chain // 2 + 1, mirror // 2 + 1
@@ -370,35 +370,27 @@
     segments.append((0, z, jnp.clip(n_own - 2 * z, 0, 2) * first_z))
     starts, final = [jnp.int32(0)], [jnp.int32(0), jnp.int32(0)]
     for k, (s, _, chunks) in enumerate(segments):
-        starts.append(starts[-1] + 2 * chunks)
+        starts.append(starts[-1] + chunks)
         final[s] = jnp.where(chunks > 0, k, final[s])
 
     def plan(t):
-        s, c, r, done = jnp.int32(0), jnp.int32(0), jnp.int32(0), jnp.int32(0)
+        s, c, done = jnp.int32(0), jnp.int32(0), jnp.int32(0)
         for k, (side, row, chunks) in enumerate(segments):
             inside = (t >= starts[k]) & (t < starts[k + 1])
-            place_in = t - starts[k]
-            pairs = chunks - 1
             s = jnp.where(inside, side, s)
-            r = jnp.where(inside, jnp.where(chunks == 2, place_in // 2, place_in), r)
-            c = jnp.where(inside, 2 * row + pairs * (place_in % 2), c)
-            ended = (final[side] == k).astype(jnp.int32) * (1 - pairs * (1 - place_in % 2))
-            done = jnp.where(inside, ended, done)
+            c = jnp.where(inside, 2 * row + t - starts[k], c)
+            ended = (final[side] == k) & (t + 1 == starts[k + 1])
+            done = jnp.where(inside, ended.astype(jnp.int32), done)
         chunks = n_own + s * (n_far - n_own)
-        return s, r, c, c == chunks - 1, done == 1
-
-    def rows_of_pass(r):
-        return pl.ds(pl.multiple_of(r * 512, 512), 512)
+        return s, c, c == chunks - 1, done == 1
 
     def score(t, dst):
-        s, r, c, _, _ = plan(t)
+        s, c, _, _ = plan(t)
         keys = kb[pl.ds(4 * c, 4)].reshape(512, KEYW)
-        dst[...] = lax.dot_general(
-            qb[s, rows_of_pass(r), :], keys, NT, preferred_element_type=jnp.float32
-        )
+        dst[...] = lax.dot_general(qb[s], keys, NT, preferred_element_type=jnp.float32)
 
     def hide(t, dst):
-        s, _, c, last, _ = plan(t)
+        s, c, last, _ = plan(t)
 
         @pl.when(last)
         def _():
@@ -421,62 +413,71 @@
         )
 
     def step(t, now, later):
-        s, r, c, _, done = plan(t)
-        rows = rows_of_pass(r)
-        score(jnp.minimum(t + 1, 17), later)
+        s, c, _, done = plan(t)
+        score(jnp.minimum(t + 1, 8), later)
         parts = [now[:, k : k + 128] * SCALE2 for k in range(0, 512, 128)]
-        before = mx[s, rows, :]
+        before = mx[s]
         top = jnp.max(functools.reduce(jnp.maximum, parts), 1, keepdims=True)
         peak = jnp.maximum(before, top)
         shrink = jnp.exp2(before - peak)
         weights = [jnp.exp2(p - peak) for p in parts]
-        mx[s, rows, :] = peak
-        tot[s, rows, :] = tot[s, rows, :] * shrink + sum(weights[1:], weights[0])
+        mx[s] = peak
+        tot[s] = tot[s] * shrink + sum(weights[1:], weights[0])
         weights = jnp.concatenate([w.astype(jnp.bfloat16) for w in weights], 1)
         latent = kb[pl.ds(4 * c, 4), :, :LAT].reshape(512, LAT)
         mixed = jnp.dot(weights, latent, preferred_element_type=jnp.float32)
         shrink = jnp.concatenate([shrink] * (LAT // 128), 1)
-        acc[s, rows, :] = acc[s, rows, :] * shrink + mixed
-        hide(jnp.minimum(t + 1, 17), later)
+        acc[s] = acc[s] * shrink + mixed
+        hide(jnp.minimum(t + 1, 8), later)
 
         @pl.when(done)
         def _():
-            for k in range(4):
-                part = pl.ds(pl.multiple_of(r * 512 + k * 128, 128), 128)
-                total = jnp.sum(tot[s, part, :], 1, keepdims=True)
-                mixed = (acc[s, part, :] * (1.0 / total)).astype(jnp.bfloat16)
-                value = jnp.dot(mixed, wv[4 * r + k], preferred_element_type=jnp.float32)
-                ob[s, :, :, part] = value.astype(jnp.bfloat16).reshape(8, 16, VH)
-
-            @pl.when(s == 1)
-            def _():
-                out_copy(r).start()
-
-            @pl.when(s == 0)
-            def _():
-                own_copy(r).start()
+            def group(r, _):
+                for k in range(4):
+                    part = pl.ds(pl.multiple_of(r * 512 + k * 128, 128), 128)
+                    total = jnp.sum(tot[s, part, :], 1, keepdims=True)
+                    mixed = (acc[s, part, :] * (1.0 / total)).astype(jnp.bfloat16)
+                    value = jnp.dot(mixed, wv[4 * r + k], preferred_element_type=jnp.float32)
+                    ob[s, :, :, part] = value.astype(jnp.bfloat16).reshape(8, 16, VH)
+
+                @pl.when(s == 1)
+                def _():
+                    out_copy(r).start()
+
+                @pl.when(s == 0)
+                def _():
+                    own_copy(r).start()
+
+                return 0
+
+            lax.fori_loop(0, 2, group, 0)
 
     loaded("wv")
     meet(z)
     score(0, first)
     hide(0, first)
 
+    def serve(t):
+        @pl.when(t + 1 == starts[2])
+        def _():
+            second_rows()
+
+        @pl.when(t + 1 == starts[6])
+        def _():
+            last_row()
+
     def two_steps(i, _):
-        for k, (now, later) in enumerate(((first, second), (second, first))):
-            t = 2 * i + k
-
-            @pl.when(t + 1 == starts[2])
-            def _():
-                second_rows()
-
-            @pl.when(t + 1 == starts[6])
-            def _():
-                last_row()
-
-            step(t, now, later)
+        serve(2 * i)
+        step(2 * i, first, second)
+
+        @pl.when(i < 4)
+        def _():
+            serve(2 * i + 1)
+            step(2 * i + 1, second, first)
+
         return 0
 
-    lax.fori_loop(0, 9, two_steps, 0)
+    lax.fori_loop(0, 5, two_steps, 0)
     for j in range(2):
         rows = pl.ds(pl.multiple_of(tp * 16, 16), 16)
         cache_ref[j] = kb[slot_ref[j], rows, :][:, :KV]
@@ -542,8 +543,8 @@
             pltpu.VMEM((2, 8, 16, QL), bf16),
             pltpu.VMEM((32, 128, KEYW), bf16),
             pltpu.VMEM((2, HEADS * 128, KEYW), bf16),
-            pltpu.VMEM((512, 512), f32),
-            pltpu.VMEM((512, 512), f32),
+            pltpu.VMEM((1024, 512), f32),
+            pltpu.VMEM((1024, 512), f32),
             pltpu.VMEM((2, HEADS * 128, LAT), f32),
             pltpu.VMEM((2, HEADS * 128, 128), f32),
             pltpu.VMEM((2, HEADS * 128, 128), f32),

time: 74.9 us -> 74.6 us (level)
  no operation moved by 1% of the time
where the time goes in v6:
time: 74.6 us; the launch traced here: 74.4 us
  Pallas kernels  73.8 us (99%)
    pallas_call x1, Pallas kernels, per_device(): pl.pallas_call(kernel, out_shape=(jax.ShapeDtypeStruct((8, 2, 16, HEADS *...  71.9 us
    pallas_call x1, Pallas kernels, per_device(): pl.pallas_call(hand_over, out_shape=(jax.ShapeDtypeStruct(attended.shape,...  1.86 us

profile of v6, /device:TPU:1, one launch (start us, length us, event | category | flops | bytes accessed | tf_op | source)
XLA Modules:
  0.0 74.4 jit_solution(8244138106917272147)
XLA Ops:
  0.6 71.9 %shard_map.113 = (bf16[8,2,16,1024]{3,2,1,0:T(8,128)(2,1)}, bf16[2,16,576]{2,1,0:T(8,128)(2,1)}) custom-call(bf16[256,896]{1,0:T(8,128)(2,1)} %tok_h.1, bf16[896,1536]{1,0:T(8,128)(2,1)} %wq_h.1, bf16[576,896]{1,0:T(8,128)(2,1)} %bitcast.4, f32[12,128]{1,0:T(8,128)} %bitcast.6, f32[4,128]{1,0:T(4,128)} %bitcast.7, bf16[1536,1536]{1,0:T(8,128)(2,1)} %wu_h.1, ...), custom_call_target="tpu_custom_call" | custom-call | tf_op jit(solution)/shard_map/pallas_call | solution.py:513
  72.6 1.9 %shard_map.114 = (bf16[256,1024]{1,0:T(8,128)(2,1)}, bf16[2,16,576]{2,1,0:T(8,128)(2,1)}) custom-call(bf16[256,1024]{1,0:T(8,128)(2,1)} %bitcast.5, bf16[2,16,576]{2,1,0:T(8,128)(2,1)} %get-tuple-element.5.cache_h), custom_call_target="tpu_custom_call" | custom-call | tf_op jit(solution)/shard_map/pallas_call | solution.py:573

commit v7 on v6

--- a/solution.py
+++ b/solution.py
@@ -320,6 +320,8 @@
     for u, v in RINGS[7:11]:
         relay(u, v)
     lax.fori_loop(HEADS // 4, HEADS // 2, expand, 0)
+    for u, v in RINGS[11:15]:
+        relay(u, v)
 
     def meet(c):
         for k in range(4):
@@ -327,13 +329,11 @@
             arrived(kb.at[2 * n + other], ks_sem.at[n])
 
     def second_rows():
-        for u, v in RINGS[11:15]:
-            relay(u, v)
+        relay(2, 2)
         meet(z + 1)
         meet(z + 3)
 
     def last_row():
-        relay(2, 2)
         meet(z + 2)
 
     def turn(n, side):

time: 74.6 us -> 74.9 us (level)
  no operation moved by 1% of the time
where the time goes in v7:
time: 74.9 us; the launch traced here: 74.7 us
  Pallas kernels  74.1 us (99%)
    pallas_call x1, Pallas kernels, per_device(): pl.pallas_call(kernel, out_shape=(jax.ShapeDtypeStruct((8, 2, 16, HEADS *...  72.2 us
    pallas_call x1, Pallas kernels, per_device(): pl.pallas_call(hand_over, out_shape=(jax.ShapeDtypeStruct(attended.shape,...  1.86 us

profile of v7, /device:TPU:1, one launch (start us, length us, event | category | flops | bytes accessed | tf_op | source)
XLA Modules:
  0.0 74.7 jit_solution(8189433065962237348)
XLA Ops:
  0.6 72.2 %shard_map.113 = (bf16[8,2,16,1024]{3,2,1,0:T(8,128)(2,1)}, bf16[2,16,576]{2,1,0:T(8,128)(2,1)}) custom-call(bf16[256,896]{1,0:T(8,128)(2,1)} %tok_h.1, bf16[896,1536]{1,0:T(8,128)(2,1)} %wq_h.1, bf16[576,896]{1,0:T(8,128)(2,1)} %bitcast.4, f32[12,128]{1,0:T(8,128)} %bitcast.6, f32[4,128]{1,0:T(4,128)} %bitcast.7, bf16[1536,1536]{1,0:T(8,128)(2,1)} %wu_h.1, ...), custom_call_target="tpu_custom_call" | custom-call | tf_op jit(solution)/shard_map/pallas_call | solution.py:513
  72.9 1.9 %shard_map.114 = (bf16[256,1024]{1,0:T(8,128)(2,1)}, bf16[2,16,576]{2,1,0:T(8,128)(2,1)}) custom-call(bf16[256,1024]{1,0:T(8,128)(2,1)} %bitcast.5, bf16[2,16,576]{2,1,0:T(8,128)(2,1)} %get-tuple-element.5.cache_h), custom_call_target="tpu_custom_call" | custom-call | tf_op jit(solution)/shard_map/pallas_call | solution.py:573

commit v8 on v1

--- a/solution.py
+++ b/solution.py
@@ -19,7 +19,7 @@
 NT = (((1,), (1,)), ((), ()))
 N_SEND = 80
 RINGS = (
-    (0, 0), (3, 0), (1, 0), (0, 3), (0, 1), (2, 0), (3, 3), (3, 1), (1, 3), (1, 1), (0, 2),
+    (0, 0), (3, 0), (1, 0), (0, 3), (0, 1), (2, 0), (0, 2), (3, 3), (3, 1), (1, 3), (1, 1),
     (2, 3), (2, 1), (3, 2), (1, 2), (2, 2),
 )
 
@@ -48,7 +48,7 @@
     out_h, cache_ref,
     tok, wq, wkv, qg, kvg, wu, wa, wv, tabk, tabq,
     psk, pok, prk, psq, poq, prq, rks, rkr, rqs, rqr, cs, cq, kb, qb, first, acc, mx, tot, ob,
-    load_sem, send_sem, sib_sem, rk_sem, rq_sem, cq_sem, ky_sem, kp_sem, ks_sem, out_sem, own_sem,
+    load_sem, send_sem, sib_sem, rk_sem, rq_sem, cq_sem, ky_sem, kp_sem, ks_sem, out_sem, outs_sem, own_sem,
 ):
     chain = lax.axis_index("chain")
     tp = lax.axis_index("tp")
@@ -85,7 +85,7 @@
         ]
     ):
         loads[name] = pltpu.make_async_copy(src, dst, load_sem.at[k])
-        if k < 6:
+        if name in ("tok", "wkv", "kvg", "tabk"):
             loads[name].start()
 
     def loaded(*names):
@@ -96,7 +96,8 @@
     partners = (sibling, up, down, pair, ap, am, bp, bm)
     for device in partners:
         pl.semaphore_signal(barrier, inc=1, device_id=device, device_id_type=MESH)
-    pl.semaphore_wait(barrier, len(partners))
+    for name in ("wq", "qg"):
+        loads[name].start()
 
     sent = []
 
@@ -167,19 +168,18 @@
 
     loaded("tok", "wkv")
     project_keys(other, psk)
+    pl.semaphore_wait(barrier, len(partners))
     send(psk, prk, sib_sem.at[0], sibling)
     project_keys(core, pok)
+    arrived(prk, sib_sem.at[0])
+    keys_start()
     loaded("wq")
     for name in ("wa", "wu", "wv", "tab0", "tab1"):
         loads[name].start()
     project_queries(other, psq)
     send(psq, prq, sib_sem.at[1], sibling)
-    arrived(prk, sib_sem.at[0])
-    keys_start()
+    keys_middle()
     project_queries(core, poq)
-    keys_middle()
-    arrived(prq, sib_sem.at[1])
-    queries_start()
 
     slot_own = 2 * chain + core
 
@@ -198,7 +198,8 @@
         ).astype(jnp.bfloat16)
     for k, device in enumerate((up, down)):
         send(keys_y(y, 0, 32), keys_y(y, 0, 32), ky_sem.at[k], device)
-    queries_middle()
+    arrived(prq, sib_sem.at[1])
+    queries_start()
     arrived(keys_y(ym, 0, 32), ky_sem.at[0])
     send(keys_y(ym, 0, 16), keys_y(ym, 0, 16), ky_sem.at[2], up)
     arrived(keys_y(yp, 0, 32), ky_sem.at[1])
@@ -242,6 +243,12 @@
     arrived(keys_y(yf, 0, 16), ky_sem.at[2])
     arrived(keys_y(yf, 1, 16), ky_sem.at[3])
     pass_on(at(0, 0), ap, am, bp, bm)
+    acc[...] = jnp.zeros_like(acc)
+    tot[...] = jnp.zeros_like(tot)
+    mx[...] = jnp.full_like(mx, FLOOR_SCORE)
+    queries_middle()
+    for u, v in RINGS[1:5]:
+        relay(u, v)
 
     loaded("qg")
     gain_q = jnp.concatenate([qg[k : k + 1, :] for k in range(QL // 128)], 1)
@@ -259,7 +266,7 @@
     cq[0, piece] = cs[half]
     give(0, piece, up, down, sibling)
     pm, pp, pf = core * 4 + ym, core * 4 + yp, core * 4 + yf
-    for u, v in RINGS[1:5]:
+    for u, v in RINGS[5:7]:
         relay(u, v)
     take(1, piece)
     give(1, piece, up, down, sibling)
@@ -267,14 +274,16 @@
     give(0, pm, up, sibling)
     take(0, pp)
     give(0, pp, sibling)
+    for u, v in RINGS[7:11]:
+        relay(u, v)
     take(1, pp)
     give(1, pp, down, sibling)
     take(1, pm)
     give(1, pm, sibling)
-    for u, v in RINGS[5:11]:
-        relay(u, v)
     take(0, pf)
     give(0, pf, sibling)
+    for u, v in RINGS[11:15]:
+        relay(u, v)
     take(1, pf)
     give(1, pf, sibling)
     for s in range(2):
@@ -302,41 +311,10 @@
                 qb[s, places, LAT:] = turned[s * 128 : s * 128 + 128]
         return 0
 
-    lax.fori_loop(0, HEADS // 4, expand, 0)
-    for u, v in RINGS[11:15]:
-        relay(u, v)
-    lax.fori_loop(HEADS // 4, HEADS // 2, expand, 0)
-    acc[...] = jnp.zeros_like(acc)
-    tot[...] = jnp.zeros_like(tot)
-    mx[...] = jnp.full_like(mx, FLOOR_SCORE)
-
-    def turn(n, side):
-        cols = pl.ds(pl.multiple_of((n % 4) * 256 + side * 128, 128), 128)
-        kt[n // 4, :LAT, cols] = kb[2 * n + side, :, :LAT].T
-
-    def turn_own(steps):
-        for u, v in steps:
-            turn(at(u, v), core)
-
-    def turn_other(steps):
-        for u, v in steps:
-            n = at(u, v)
-            arrived(kb.at[2 * n + other], ks_sem.at[n])
-            turn(n, other)
-
-    def whole(n):
-        arrived(block(n), kp_sem.at[n, 0])
-
-    def halves(n):
-        for p in range(2):
-            arrived(block(n, p), kp_sem.at[n, p])
-
+    lax.fori_loop(0, HEADS // 2, expand, 0)
     relay(2, 2)
     for n in range(16):
         arrived(kb.at[2 * n + other], ks_sem.at[n])
-    for j in range(2):
-        rows = pl.ds(pl.multiple_of(tp * 16, 16), 16)
-        cache_ref[j] = kb[slot_ref[j], rows, :][:, :KV]
 
     token = lax.broadcasted_iota(jnp.int32, (512, 1), 0) & 127
     place = ((token >> 4) << 5) + (token & 15) + half * 16
@@ -390,27 +368,45 @@
         def _():
             chunk(s, blk // 4, blk, 512, True)
 
+    def out_cols(r):
+        return pl.ds(pl.multiple_of(r * 512, 512), 512)
+
+    def out_copy(r):
+        return pltpu.make_async_remote_copy(
+            src_ref=ob.at[1, :, :, out_cols(r)], dst_ref=out_h.at[:, half, :, out_cols(r)],
+            send_sem=outs_sem.at[r], recv_sem=out_sem.at[r], device_id=pair, device_id_type=MESH,
+        )
+
+    def own_copy(r):
+        return pltpu.make_async_copy(
+            ob.at[0, :, :, out_cols(r)], out_h.at[:, half, :, out_cols(r)], own_sem.at[r]
+        )
+
     def finish(s):
-        def value_of(h, _):
-            cols = pl.ds(pl.multiple_of(h * VH, VH), VH)
-            total = jnp.sum(tot[s, cols, :], 1, keepdims=True)
-            mixed = (acc[s, cols, :] * (1.0 / total)).astype(jnp.bfloat16)
-            value = jnp.dot(mixed, wv[h], preferred_element_type=jnp.float32)
-            ob[s, :, :, cols] = value.astype(jnp.bfloat16).reshape(8, 16, VH)
+        def group(r, _):
+            for k in range(4):
+                part = pl.ds(pl.multiple_of(r * 512 + k * 128, 128), 128)
+                total = jnp.sum(tot[s, part, :], 1, keepdims=True)
+                mixed = (acc[s, part, :] * (1.0 / total)).astype(jnp.bfloat16)
+                value = jnp.dot(mixed, wv[4 * r + k], preferred_element_type=jnp.float32)
+                ob[s, :, :, part] = value.astype(jnp.bfloat16).reshape(8, 16, VH)
+            (own_copy, out_copy)[s](r).start()
             return 0
 
-        lax.fori_loop(0, HEADS, value_of, 0)
-
+        lax.fori_loop(0, 2, group, 0)
+
+    loaded("wv")
     attend(1, mirror)
-    loaded("wv")
     finish(1)
-    send(ob.at[1], out_h.at[:, half], out_sem.at[0], pair)
     attend(0, chain)
     finish(0)
-    keep = pltpu.make_async_copy(ob.at[0], out_h.at[:, half], own_sem.at[0])
-    keep.start()
-    keep.wait()
-    arrived(out_h.at[:, 1 - half], out_sem.at[0])
+    for j in range(2):
+        rows = pl.ds(pl.multiple_of(tp * 16, 16), 16)
+        cache_ref[j] = kb[slot_ref[j], rows, :][:, :KV]
+    for r in range(2):
+        own_copy(r).wait()
+        out_copy(r).wait_send()
+        arrived(out_h.at[:, 1 - half, :, out_cols(r)], out_sem.at[r])
     for copy in sent:
         copy.wait_send()
 
@@ -483,8 +479,9 @@
             dma((4,)),
             dma((16, 2)),
             dma((16,)),
-            dma((1,)),
-            dma((1,)),
+            dma((2,)),
+            dma((2,)),
+            dma((2,)),
         ],
         compiler_params=pltpu.CompilerParams(
             collective_id=0, has_side_effects=True, vmem_limit_bytes=56 * 2**20

time: 74.4 us -> 74.8 us (level); the launches traced: 74.3 us -> 73.6 us
  no operation moved by 1% of the time
where the time goes in v8:
time: 74.8 us; the launch traced here: 73.6 us
  Pallas kernels  72.8 us (97%)
  between operations  0.8 us (1%)
    pallas_call x1, Pallas kernels, per_device(): pl.pallas_call(kernel, out_shape=(jax.ShapeDtypeStruct((8, 2, 16, HEADS *...  70.9 us
    pallas_call x1, Pallas kernels, per_device(): pl.pallas_call(hand_over, out_shape=(jax.ShapeDtypeStruct(attended.shape,...  1.86 us

profile of v8, /device:TPU:1, one launch (start us, length us, event | category | flops | bytes accessed | tf_op | source)
XLA Modules:
  0.0 73.6 jit_solution(10392906497500724443)
XLA Ops:
  0.6 70.9 %shard_map.113 = (bf16[8,2,16,1024]{3,2,1,0:T(8,128)(2,1)}, bf16[2,16,576]{2,1,0:T(8,128)(2,1)}) custom-call(bf16[256,896]{1,0:T(8,128)(2,1)} %tok_h.1, bf16[896,1536]{1,0:T(8,128)(2,1)} %wq_h.1, bf16[576,896]{1,0:T(8,128)(2,1)} %bitcast.4, f32[12,128]{1,0:T(8,128)} %bitcast.6, f32[4,128]{1,0:T(4,128)} %bitcast.7, bf16[1536,1536]{1,0:T(8,128)(2,1)} %wu_h.1, ...), custom_call_target="tpu_custom_call" | custom-call | tf_op jit(solution)/shard_map/pallas_call | solution.py:435
  71.6 1.9 %shard_map.114 = (bf16[256,1024]{1,0:T(8,128)(2,1)}, bf16[2,16,576]{2,1,0:T(8,128)(2,1)}) custom-call(bf16[256,1024]{1,0:T(8,128)(2,1)} %bitcast.5, bf16[2,16,576]{2,1,0:T(8,128)(2,1)} %get-tuple-element.5.cache_h), custom_call_target="tpu_custom_call" | custom-call | tf_op jit(solution)/shard_map/pallas_call | solution.py:494

commit v9 on v8

--- a/solution.py
+++ b/solution.py
@@ -180,6 +180,8 @@
     send(psq, prq, sib_sem.at[1], sibling)
     keys_middle()
     project_queries(core, poq)
+    arrived(prq, sib_sem.at[1])
+    queries_start()
 
     slot_own = 2 * chain + core
 
@@ -198,8 +200,6 @@
         ).astype(jnp.bfloat16)
     for k, device in enumerate((up, down)):
         send(keys_y(y, 0, 32), keys_y(y, 0, 32), ky_sem.at[k], device)
-    arrived(prq, sib_sem.at[1])
-    queries_start()
     arrived(keys_y(ym, 0, 32), ky_sem.at[0])
     send(keys_y(ym, 0, 16), keys_y(ym, 0, 16), ky_sem.at[2], up)
     arrived(keys_y(yp, 0, 32), ky_sem.at[1])
@@ -247,8 +247,6 @@
     tot[...] = jnp.zeros_like(tot)
     mx[...] = jnp.full_like(mx, FLOOR_SCORE)
     queries_middle()
-    for u, v in RINGS[1:5]:
-        relay(u, v)
 
     loaded("qg")
     gain_q = jnp.concatenate([qg[k : k + 1, :] for k in range(QL // 128)], 1)
@@ -266,7 +264,7 @@
     cq[0, piece] = cs[half]
     give(0, piece, up, down, sibling)
     pm, pp, pf = core * 4 + ym, core * 4 + yp, core * 4 + yf
-    for u, v in RINGS[5:7]:
+    for u, v in RINGS[1:7]:
         relay(u, v)
     take(1, piece)
     give(1, piece, up, down, sibling)
@@ -313,8 +311,13 @@
 
     lax.fori_loop(0, HEADS // 2, expand, 0)
     relay(2, 2)
-    for n in range(16):
-        arrived(kb.at[2 * n + other], ks_sem.at[n])
+
+    def meet(c):
+        for k in range(4):
+            n = 4 * c + k
+            arrived(kb.at[2 * n + other], ks_sem.at[n])
+
+    meet(0)
 
     token = lax.broadcasted_iota(jnp.int32, (512, 1), 0) & 127
     place = ((token >> 4) << 5) + (token & 15) + half * 16
@@ -334,6 +337,8 @@
                 ahead = score(s, c, r + 1, size)
             elif not last:
                 first[...] = score(s, c + 1, 0, size)
+            elif s == 1:
+                first[...] = score(0, 0, 0, 1024)
             if last:
                 visible = key_iota[:, :size] + 1024 * c <= place + 256 * blk
                 scores = jnp.where(visible, scores, FLOOR_SCORE)
@@ -351,22 +356,20 @@
             shrink = jnp.concatenate([shrink] * (LAT // 128), 1)
             acc[s, rows, :] = acc[s, rows, :] * shrink + mixed
 
-    def attend(s, blk):
-        first[...] = score(s, 0, 0, 1024)
-
+    def attend(s, blk, met):
         def step(c, _):
+            @pl.when(c + 1 > met)
+            def _():
+                meet(c + 1)
+
             chunk(s, c, blk, 1024, False)
             return 0
 
         lax.fori_loop(0, blk // 4, step, 0)
-
-        @pl.when(blk % 4 >= 2)
-        def _():
-            chunk(s, blk // 4, blk, 1024, True)
-
-        @pl.when(blk % 4 < 2)
-        def _():
-            chunk(s, blk // 4, blk, 512, True)
+        for k in range(4):
+            @pl.when(blk % 4 == k)
+            def _():
+                chunk(s, blk // 4, blk, 256 * k + 256, True)
 
     def out_cols(r):
         return pl.ds(pl.multiple_of(r * 512, 512), 512)
@@ -396,10 +399,17 @@
         lax.fori_loop(0, 2, group, 0)
 
     loaded("wv")
-    attend(1, mirror)
+    first[...] = score(1, 0, 0, 1024)
+    attend(1, mirror, 0)
     finish(1)
-    attend(0, chain)
+    attend(0, chain, 3 - z)
     finish(0)
+
+    def rest(c, _):
+        meet(c)
+        return 0
+
+    lax.fori_loop(jnp.maximum(3 - z, z) + 1, 4, rest, 0)
     for j in range(2):
         rows = pl.ds(pl.multiple_of(tp * 16, 16), 16)
         cache_ref[j] = kb[slot_ref[j], rows, :][:, :KV]

time: 74.8 us -> 75 us (level); the launches traced: 73.6 us -> 74.9 us
  Pallas kernels: 72.8 us -> 74.1 us
    pallas_call x1, Pallas kernels: 70.9 us -> 72.2 us  [per_device(): pl.pallas_call(kernel, out_shape=(jax.ShapeDtypeStruct((8, 2, 16, HEADS *...]
where the time goes in v9:
time: 75 us; the launch traced here: 74.9 us
  Pallas kernels  74.1 us (99%)
  between operations  0.82 us (1%)
    pallas_call x1, Pallas kernels, per_device(): pl.pallas_call(kernel, out_shape=(jax.ShapeDtypeStruct((8, 2, 16, HEADS *...  72.2 us
    pallas_call x1, Pallas kernels, per_device(): pl.pallas_call(hand_over, out_shape=(jax.ShapeDtypeStruct(attended.shape,...  1.86 us

profile of v9, /device:TPU:1, one launch (start us, length us, event | category | flops | bytes accessed | tf_op | source)
XLA Modules:
  0.0 74.9 jit_solution(11552310446101383737)
XLA Ops:
  0.6 72.2 %shard_map.113 = (bf16[8,2,16,1024]{3,2,1,0:T(8,128)(2,1)}, bf16[2,16,576]{2,1,0:T(8,128)(2,1)}) custom-call(bf16[256,896]{1,0:T(8,128)(2,1)} %tok_h.1, bf16[896,1536]{1,0:T(8,128)(2,1)} %wq_h.1, bf16[576,896]{1,0:T(8,128)(2,1)} %bitcast.4, f32[12,128]{1,0:T(8,128)} %bitcast.6, f32[4,128]{1,0:T(4,128)} %bitcast.7, bf16[1536,1536]{1,0:T(8,128)(2,1)} %wu_h.1, ...), custom_call_target="tpu_custom_call" | custom-call | tf_op jit(solution)/shard_map/pallas_call | solution.py:445
  72.9 1.9 %shard_map.114 = (bf16[256,1024]{1,0:T(8,128)(2,1)}, bf16[2,16,576]{2,1,0:T(8,128)(2,1)}) custom-call(bf16[256,1024]{1,0:T(8,128)(2,1)} %bitcast.5, bf16[2,16,576]{2,1,0:T(8,128)(2,1)} %get-tuple-element.5.cache_h), custom_call_target="tpu_custom_call" | custom-call | tf_op jit(solution)/shard_map/pallas_call | solution.py:504

commit v10 on v9

--- a/solution.py
+++ b/solution.py
@@ -323,53 +323,49 @@
     place = ((token >> 4) << 5) + (token & 15) + half * 16
     key_iota = lax.broadcasted_iota(jnp.int32, (1, 1024), 1)
 
-    def score(s, c, r, size):
-        keys = kb[pl.ds(8 * c, size // 128)].reshape(size, KEYW)
-        queries = qb[s, 512 * r : 512 * r + 512, :]
+    def score(s, c, r):
+        keys = kb[pl.ds(8 * c, 8)].reshape(1024, KEYW)
+        queries = qb[s, pl.ds(pl.multiple_of(r * 512, 512), 512), :]
         return lax.dot_general(queries, keys, NT, preferred_element_type=jnp.float32)
 
-    def chunk(s, c, blk, size, last):
-        ahead = first[:, :size]
-        for r in range(2):
-            rows = slice(512 * r, 512 * r + 512)
-            scores = ahead * SCALE2
-            if r < 1:
-                ahead = score(s, c, r + 1, size)
-            elif not last:
-                first[...] = score(s, c + 1, 0, size)
-            elif s == 1:
-                first[...] = score(0, 0, 0, 1024)
-            if last:
-                visible = key_iota[:, :size] + 1024 * c <= place + 256 * blk
-                scores = jnp.where(visible, scores, FLOOR_SCORE)
-            parts = [scores[:, k : k + 128] for k in range(0, size, 128)]
-            before = mx[s, rows, :]
-            top = jnp.max(functools.reduce(jnp.maximum, parts), 1, keepdims=True)
-            peak = jnp.maximum(before, top)
-            shrink = jnp.exp2(before - peak)
-            weights = [jnp.exp2(p - peak) for p in parts]
-            mx[s, rows, :] = peak
-            tot[s, rows, :] = tot[s, rows, :] * shrink + sum(weights[1:], weights[0])
-            weights = jnp.concatenate([w.astype(jnp.bfloat16) for w in weights], 1)
-            latent = kb[pl.ds(8 * c, size // 128), :, :LAT].reshape(size, LAT)
-            mixed = jnp.dot(weights, latent, preferred_element_type=jnp.float32)
-            shrink = jnp.concatenate([shrink] * (LAT // 128), 1)
-            acc[s, rows, :] = acc[s, rows, :] * shrink + mixed
-
-    def attend(s, blk, met):
+    def tile(s, r, c, blk, size, last, following):
+        rows = pl.ds(pl.multiple_of(r * 512, 512), 512)
+        scores = first[:, :size] * SCALE2
+        if following is not None:
+            first[...] = score(*following)
+        if last:
+            visible = key_iota[:, :size] + 1024 * c <= place + 256 * blk
+            scores = jnp.where(visible, scores, FLOOR_SCORE)
+        parts = [scores[:, k : k + 128] for k in range(0, size, 128)]
+        before = mx[s, rows, :]
+        top = jnp.max(functools.reduce(jnp.maximum, parts), 1, keepdims=True)
+        peak = jnp.maximum(before, top)
+        shrink = jnp.exp2(before - peak)
+        weights = [jnp.exp2(p - peak) for p in parts]
+        mx[s, rows, :] = peak
+        tot[s, rows, :] = tot[s, rows, :] * shrink + sum(weights[1:], weights[0])
+        weights = jnp.concatenate([w.astype(jnp.bfloat16) for w in weights], 1)
+        latent = kb[pl.ds(8 * c, size // 128), :, :LAT].reshape(size, LAT)
+        mixed = jnp.dot(weights, latent, preferred_element_type=jnp.float32)
+        shrink = jnp.concatenate([shrink] * (LAT // 128), 1)
+        acc[s, rows, :] = acc[s, rows, :] * shrink + mixed
+
+    def attend(s, r, blk, met, after):
         def step(c, _):
             @pl.when(c + 1 > met)
             def _():
                 meet(c + 1)
 
-            chunk(s, c, blk, 1024, False)
+            tile(s, r, c, blk, 1024, False, (s, c + 1, r))
             return 0
 
         lax.fori_loop(0, blk // 4, step, 0)
         for k in range(4):
             @pl.when(blk % 4 == k)
             def _():
-                chunk(s, blk // 4, blk, 256 * k + 256, True)
+                tile(s, r, blk // 4, blk, 256 * k + 256, True, after)
+
+        finish(s, r)
 
     def out_cols(r):
         return pl.ds(pl.multiple_of(r * 512, 512), 512)
@@ -385,25 +381,25 @@
             ob.at[0, :, :, out_cols(r)], out_h.at[:, half, :, out_cols(r)], own_sem.at[r]
         )
 
-    def finish(s):
-        def group(r, _):
-            for k in range(4):
-                part = pl.ds(pl.multiple_of(r * 512 + k * 128, 128), 128)
-                total = jnp.sum(tot[s, part, :], 1, keepdims=True)
-                mixed = (acc[s, part, :] * (1.0 / total)).astype(jnp.bfloat16)
-                value = jnp.dot(mixed, wv[4 * r + k], preferred_element_type=jnp.float32)
-                ob[s, :, :, part] = value.astype(jnp.bfloat16).reshape(8, 16, VH)
-            (own_copy, out_copy)[s](r).start()
-            return 0
-
-        lax.fori_loop(0, 2, group, 0)
+    def finish(s, r):
+        for k in range(4):
+            part = pl.ds(pl.multiple_of(r * 512 + k * 128, 128), 128)
+            total = jnp.sum(tot[s, part, :], 1, keepdims=True)
+            mixed = (acc[s, part, :] * (1.0 / total)).astype(jnp.bfloat16)
+            value = jnp.dot(mixed, wv[4 * r + k], preferred_element_type=jnp.float32)
+            ob[s, :, :, part] = value.astype(jnp.bfloat16).reshape(8, 16, VH)
+        (own_copy, out_copy)[s](r).start()
 
     loaded("wv")
-    first[...] = score(1, 0, 0, 1024)
-    attend(1, mirror, 0)
-    finish(1)
-    attend(0, chain, 3 - z)
-    finish(0)
+    first[...] = score(1, 0, 0)
+
+    def far_pass(r, _):
+        attend(1, r, mirror, r * (3 - z), (1 - r, 0, 1 - r))
+        return 0
+
+    lax.fori_loop(0, 2, far_pass, 0)
+    attend(0, 0, chain, 3 - z, (0, 0, 1))
+    attend(0, 1, chain, 3, None)
 
     def rest(c, _):
         meet(c)

time: 75 us -> 73.6 us (0.981)
  Pallas kernels: 74.1 us -> 72.6 us
    pallas_call x1, Pallas kernels: 72.2 us -> 70.8 us  [per_device(): pl.pallas_call(kernel, out_shape=(jax.ShapeDtypeStruct((8, 2, 16, HEADS *...]
where the time goes in v10:
time: 73.6 us; the launch traced here: 73.4 us
  Pallas kernels  72.6 us (99%)
  between operations  0.8 us (1%)
    pallas_call x1, Pallas kernels, per_device(): pl.pallas_call(kernel, out_shape=(jax.ShapeDtypeStruct((8, 2, 16, HEADS *...  70.8 us
    pallas_call x1, Pallas kernels, per_device(): pl.pallas_call(hand_over, out_shape=(jax.ShapeDtypeStruct(attended.shape,...  1.86 us

profile of v10, /device:TPU:1, one launch (start us, length us, event | category | flops | bytes accessed | tf_op | source)
XLA Modules:
  0.0 73.4 jit_solution(5193243443189794397)
XLA Ops:
  0.6 70.8 %shard_map.113 = (bf16[8,2,16,1024]{3,2,1,0:T(8,128)(2,1)}, bf16[2,16,576]{2,1,0:T(8,128)(2,1)}) custom-call(bf16[256,896]{1,0:T(8,128)(2,1)} %tok_h.1, bf16[896,1536]{1,0:T(8,128)(2,1)} %wq_h.1, bf16[576,896]{1,0:T(8,128)(2,1)} %bitcast.4, f32[12,128]{1,0:T(8,128)} %bitcast.6, f32[4,128]{1,0:T(4,128)} %bitcast.7, bf16[1536,1536]{1,0:T(8,128)(2,1)} %wu_h.1, ...), custom_call_target="tpu_custom_call" | custom-call | tf_op jit(solution)/shard_map/pallas_call | solution.py:441
  71.4 1.9 %shard_map.114 = (bf16[256,1024]{1,0:T(8,128)(2,1)}, bf16[2,16,576]{2,1,0:T(8,128)(2,1)}) custom-call(bf16[256,1024]{1,0:T(8,128)(2,1)} %bitcast.5, bf16[2,16,576]{2,1,0:T(8,128)(2,1)} %get-tuple-element.5.cache_h), custom_call_target="tpu_custom_call" | custom-call | tf_op jit(solution)/shard_map/pallas_call | solution.py:500

commit v11 on v10

--- a/solution.py
+++ b/solution.py
@@ -264,7 +264,7 @@
     cq[0, piece] = cs[half]
     give(0, piece, up, down, sibling)
     pm, pp, pf = core * 4 + ym, core * 4 + yp, core * 4 + yf
-    for u, v in RINGS[1:7]:
+    for u, v in RINGS[1:5]:
         relay(u, v)
     take(1, piece)
     give(1, piece, up, down, sibling)
@@ -272,18 +272,20 @@
     give(0, pm, up, sibling)
     take(0, pp)
     give(0, pp, sibling)
-    for u, v in RINGS[7:11]:
+    for u, v in RINGS[5:7]:
         relay(u, v)
     take(1, pp)
     give(1, pp, down, sibling)
     take(1, pm)
     give(1, pm, sibling)
+    for u, v in RINGS[7:11]:
+        relay(u, v)
     take(0, pf)
     give(0, pf, sibling)
+    take(1, pf)
+    give(1, pf, sibling)
     for u, v in RINGS[11:15]:
         relay(u, v)
-    take(1, pf)
-    give(1, pf, sibling)
     for s in range(2):
         for yy in range(4):
             take(s, other * 4 + yy)

time: 73.6 us -> 71.2 us (0.967)
  Pallas kernels: 72.6 us -> 70.2 us
    pallas_call x1, Pallas kernels: 70.8 us -> 68.3 us  [per_device(): pl.pallas_call(kernel, out_shape=(jax.ShapeDtypeStruct((8, 2, 16, HEADS *...]
where the time goes in v11:
time: 71.2 us; the launch traced here: 71 us
  Pallas kernels  70.2 us (99%)
  between operations  0.8 us (1%)
    pallas_call x1, Pallas kernels, per_device(): pl.pallas_call(kernel, out_shape=(jax.ShapeDtypeStruct((8, 2, 16, HEADS *...  68.3 us
    pallas_call x1, Pallas kernels, per_device(): pl.pallas_call(hand_over, out_shape=(jax.ShapeDtypeStruct(attended.shape,...  1.86 us

profile of v11, /device:TPU:1, one launch (start us, length us, event | category | flops | bytes accessed | tf_op | source)
XLA Modules:
  0.0 71.0 jit_solution(7064757321256660459)
XLA Ops:
  0.6 68.3 %shard_map.113 = (bf16[8,2,16,1024]{3,2,1,0:T(8,128)(2,1)}, bf16[2,16,576]{2,1,0:T(8,128)(2,1)}) custom-call(bf16[256,896]{1,0:T(8,128)(2,1)} %tok_h.1, bf16[896,1536]{1,0:T(8,128)(2,1)} %wq_h.1, bf16[576,896]{1,0:T(8,128)(2,1)} %bitcast.4, f32[12,128]{1,0:T(8,128)} %bitcast.6, f32[4,128]{1,0:T(4,128)} %bitcast.7, bf16[1536,1536]{1,0:T(8,128)(2,1)} %wu_h.1, ...), custom_call_target="tpu_custom_call" | custom-call | tf_op jit(solution)/shard_map/pallas_call | solution.py:443
  69.0 1.9 %shard_map.114 = (bf16[256,1024]{1,0:T(8,128)(2,1)}, bf16[2,16,576]{2,1,0:T(8,128)(2,1)}) custom-call(bf16[256,1024]{1,0:T(8,128)(2,1)} %bitcast.5, bf16[2,16,576]{2,1,0:T(8,128)(2,1)} %get-tuple-element.5.cache_h), custom_call_target="tpu_custom_call" | custom-call | tf_op jit(solution)/shard_map/pallas_call | solution.py:502

commit v12 on v11

--- a/solution.py
+++ b/solution.py
@@ -272,10 +272,10 @@
     give(0, pm, up, sibling)
     take(0, pp)
     give(0, pp, sibling)
+    take(1, pp)
+    give(1, pp, down, sibling)
     for u, v in RINGS[5:7]:
         relay(u, v)
-    take(1, pp)
-    give(1, pp, down, sibling)
     take(1, pm)
     give(1, pm, sibling)
     for u, v in RINGS[7:11]:

time: 71.2 us -> 71.2 us (level)
  no operation moved by 1% of the time
where the time goes in v12:
time: 71.2 us; the launch traced here: 70.8 us
  Pallas kernels  70 us (98%)
  between operations  0.8 us (1%)
    pallas_call x1, Pallas kernels, per_device(): pl.pallas_call(kernel, out_shape=(jax.ShapeDtypeStruct((8, 2, 16, HEADS *...  68.2 us
    pallas_call x1, Pallas kernels, per_device(): pl.pallas_call(hand_over, out_shape=(jax.ShapeDtypeStruct(attended.shape,...  1.86 us

profile of v12, /device:TPU:1, one launch (start us, length us, event | category | flops | bytes accessed | tf_op | source)
XLA Modules:
  0.0 70.8 jit_solution(12189741044183297298)
XLA Ops:
  0.6 68.2 %shard_map.113 = (bf16[8,2,16,1024]{3,2,1,0:T(8,128)(2,1)}, bf16[2,16,576]{2,1,0:T(8,128)(2,1)}) custom-call(bf16[256,896]{1,0:T(8,128)(2,1)} %tok_h.1, bf16[896,1536]{1,0:T(8,128)(2,1)} %wq_h.1, bf16[576,896]{1,0:T(8,128)(2,1)} %bitcast.4, f32[12,128]{1,0:T(8,128)} %bitcast.6, f32[4,128]{1,0:T(4,128)} %bitcast.7, bf16[1536,1536]{1,0:T(8,128)(2,1)} %wu_h.1, ...), custom_call_target="tpu_custom_call" | custom-call | tf_op jit(solution)/shard_map/pallas_call | solution.py:443
  68.8 1.9 %shard_map.114 = (bf16[256,1024]{1,0:T(8,128)(2,1)}, bf16[2,16,576]{2,1,0:T(8,128)(2,1)}) custom-call(bf16[256,1024]{1,0:T(8,128)(2,1)} %bitcast.5, bf16[2,16,576]{2,1,0:T(8,128)(2,1)} %get-tuple-element.5.cache_h), custom_call_target="tpu_custom_call" | custom-call | tf_op jit(solution)/shard_map/pallas_call | solution.py:502
